TPU v7x, 256 devices: a whole 4x4x8 slice. The times are simulated.
256 devices in a mesh: frame: 8 (over z_hi, y), height: 4 (over z_lo), width: 8 (over x, core).
Axes of the slice: x: 4, y: 4, z: 8 (z_hi: 2, z_lo: 4; z = z_hi * 4 + z_lo), core: 2. Of those that a mesh axis runs over, the one named last changes fastest.
Arguments:
- queries: bfloat16 [32, 24, 48, 1536], P('frame', 'height', 'width'), may hold values from -6 to 6
- keys: bfloat16 [32, 24, 48, 1536], P('frame', 'height', 'width'), may hold values from -6 to 6
- values: bfloat16 [32, 24, 48, 1536], P('frame', 'height', 'width'), may hold values from -6 to 6
- out_grad: bfloat16 [32, 24, 48, 1536], P('frame', 'height', 'width'), may hold values from -6 to 6
- extents: int32 [12, 3], replicated, may hold values from 1 to 2, as said below
Outputs:
- attended: bfloat16 [32, 24, 48, 1536], P('frame', 'height', 'width')
- query_grad: bfloat16 [32, 24, 48, 1536], P('frame', 'height', 'width')
- key_grad: bfloat16 [32, 24, 48, 1536], P('frame', 'height', 'width')
- value_grad: bfloat16 [32, 24, 48, 1536], P('frame', 'height', 'width')
Inputs may be any that keep to these rules, and one draw needn't show every extreme that they name: `extents`: some head has 2 on all three axes.
All inputs are finite; a program needn't handle non-finite values.
Results may differ from a plain program's by a relative error of at most 0.0062.
Values may be sent and summed in bfloat16 or wider, within the bound.
A program may use at most 128 MiB of HBM per device.

v0:
```python
import jax
import jax.numpy as jnp
from jax import lax
from jax.sharding import PartitionSpec as P

HEADS = 12
HD = 128
EXT = 2


def extended(cells, sides, width):
    for axis, dim in sides:
        count = lax.axis_size(axis)
        ends = count - 1
        head = lax.slice_in_dim(cells, 0, width, axis=dim)
        tail = lax.slice_in_dim(cells, cells.shape[dim] - width, cells.shape[dim], axis=dim)
        cells = jnp.concatenate(
            [
                lax.ppermute(tail, axis, [(i, (i + 1) % count) for i in range(ends)]),
                cells,
                lax.ppermute(head, axis, [((i + 1) % count, i) for i in range(ends)]),
            ],
            axis=dim,
        )
    return cells


def passed_along(block, axis, distance):
    devices = range(lax.axis_size(axis))
    route = [(i - distance, i) for i in devices if i - distance in devices]
    return lax.ppermute(block, axis, route)


def dot_rows(left, right):
    return lax.dot_general(
        left, right, (((1,), (1,)), ((), ())), preferred_element_type=jnp.float32
    )


def dot_cols(left, right):
    return lax.dot_general(
        left, right, (((0,), (0,)), ((), ())), preferred_element_type=jnp.float32
    )


def split_heads(flat):
    count = flat.shape[0]
    return flat.reshape(count, HEADS, HD).transpose(1, 0, 2)


def merge_heads(stacked, dims):
    return stacked.transpose(1, 0, 2).reshape(tuple(dims) + (HEADS * HD,))


def positions(anchor, dims):
    result = []
    for which in range(3):
        ramp = lax.broadcasted_iota(jnp.int32, tuple(dims), which)
        result.append((anchor[which] + ramp).reshape(-1))
    return tuple(result)


def make_mask(near_pos, far_pos, reach, grid):
    keep = jnp.ones((near_pos[0].shape[0], far_pos[0].shape[0]), dtype=bool)
    for which in range(3):
        near_axis = near_pos[which]
        far_axis = far_pos[which]
        inside = (far_axis >= 0) & (far_axis < grid[which])
        keep = (
            keep
            & (jnp.abs(far_axis[None, :] - near_axis[:, None]) <= reach[which])
            & inside[None, :]
        )
    return keep


def forward_tile(query_tile, key_box, anchor, extents, grid):
    tile_dims = query_tile.shape[:3]
    box_dims = key_box.shape[:3]
    chans = query_tile.shape[3]
    count = tile_dims[0] * tile_dims[1] * tile_dims[2]
    box_count = box_dims[0] * box_dims[1] * box_dims[2]
    score_scale = HD ** (-0.5)
    query_heads = split_heads(query_tile.reshape(count, chans))
    flat_box = key_box.reshape(box_count, 2 * chans)
    key_heads = split_heads(flat_box[:, :chans])
    value_heads = split_heads(flat_box[:, chans:])
    query_pos = positions(anchor, tile_dims)
    key_pos = positions(tuple((value - EXT for value in anchor)), box_dims)

    def forward_one_head(inputs):
        query_one, key_one, value_one, reach = inputs
        keep = make_mask(query_pos, key_pos, reach, grid)
        scores = jnp.where(keep, dot_rows(query_one, key_one) * score_scale, -1e30)
        top_score = scores.max(axis=1, keepdims=True)
        log_total = top_score + jnp.log(jnp.sum(jnp.exp(scores - top_score), axis=1, keepdims=True))
        probs = jnp.where(keep, jnp.exp(scores - log_total), 0.0)
        return (
            jnp.dot(probs.astype(jnp.bfloat16), value_one, preferred_element_type=jnp.float32),
            log_total[:, 0],
        )

    head_outs, log_totals = lax.map(
        forward_one_head, (query_heads, key_heads, value_heads, extents)
    )
    return (
        merge_heads(head_outs, tile_dims).astype(jnp.bfloat16),
        log_totals.T.reshape(tuple(tile_dims) + (HEADS,)),
    )


def query_backward(query_tile, grad_tile, lse_tile, delta_tile, key_box, anchor, extents, grid):
    tile_dims = query_tile.shape[:3]
    box_dims = key_box.shape[:3]
    chans = query_tile.shape[3]
    count = tile_dims[0] * tile_dims[1] * tile_dims[2]
    box_count = box_dims[0] * box_dims[1] * box_dims[2]
    score_scale = HD ** (-0.5)
    query_heads = split_heads(query_tile.reshape(count, chans))
    grad_heads = split_heads(grad_tile.reshape(count, chans))
    lse_heads = lse_tile.reshape(count, HEADS).T
    delta_heads = delta_tile.reshape(count, HEADS).T
    flat_box = key_box.reshape(box_count, 2 * chans)
    key_heads = split_heads(flat_box[:, :chans])
    value_heads = split_heads(flat_box[:, chans:])
    query_pos = positions(anchor, tile_dims)
    key_pos = positions(tuple((value - EXT for value in anchor)), box_dims)

    def query_one_head(inputs):
        query_one, grad_one, lse_one, delta_one, key_one, value_one, reach = inputs
        keep = make_mask(query_pos, key_pos, reach, grid)
        scores = dot_rows(query_one, key_one) * score_scale
        probs = jnp.where(keep, jnp.exp(scores - lse_one[:, None]), 0.0)
        dprobs = dot_rows(grad_one, value_one)
        dscores = (probs * (dprobs - delta_one[:, None]) * score_scale).astype(jnp.bfloat16)
        query_part = jnp.dot(dscores, key_one, preferred_element_type=jnp.float32)
        key_part = dot_cols(dscores, query_one)
        value_part = dot_cols(probs.astype(jnp.bfloat16), grad_one)
        return (query_part, key_part, value_part)

    results = lax.map(
        query_one_head,
        (query_heads, grad_heads, lse_heads, delta_heads, key_heads, value_heads, extents),
    )
    query_parts, key_parts, value_parts = results
    partial_box = jnp.concatenate(
        [merge_heads(key_parts, box_dims), merge_heads(value_parts, box_dims)], axis=-1
    )
    return (merge_heads(query_parts, tile_dims).astype(jnp.bfloat16), partial_box)


def row_products(out_grad, attended):
    joined = out_grad.astype(jnp.float32) * attended.astype(jnp.float32)
    return joined.reshape(joined.shape[:3] + (HEADS, HD)).sum(axis=-1)


def add_rims(middle, head_add, tail_add, dim):
    extra = middle.shape[dim] - EXT
    head_pad = [(0, 0)] * middle.ndim
    tail_pad = [(0, 0)] * middle.ndim
    head_pad[dim] = (0, extra)
    tail_pad[dim] = (extra, 0)
    return middle + jnp.pad(head_add, head_pad) + jnp.pad(tail_add, tail_pad)


def split_rims(partial_value, dim):
    length = partial_value.shape[dim]
    lower = lax.slice_in_dim(partial_value, 0, EXT, axis=dim)
    upper = lax.slice_in_dim(partial_value, length - EXT, length, axis=dim)
    middle = lax.slice_in_dim(partial_value, EXT, length - EXT, axis=dim)
    return (lower, middle, upper)


def on_device(queries, keys, values, out_grad, extents):
    frame_len, row_len, col_len, chans = queries.shape
    grid = (
        lax.axis_size("frame") * frame_len,
        lax.axis_size("height") * row_len,
        lax.axis_size("width") * col_len,
    )
    anchor = (
        lax.axis_index("frame") * frame_len,
        lax.axis_index("height") * row_len,
        lax.axis_index("width") * col_len,
    )
    joined_kv = jnp.concatenate([keys, values], axis=-1)
    key_box = extended(joined_kv, (("frame", 0), ("height", 1), ("width", 2)), EXT)
    attended, lse = forward_tile(queries, key_box, anchor, extents, grid)
    delta = row_products(out_grad, attended)
    query_grad, partial_value = query_backward(
        queries, out_grad, lse, delta, key_box, anchor, extents, grid
    )
    lower, middle, upper = split_rims(partial_value, 0)
    from_below = passed_along(upper, "frame", 1)
    from_above = passed_along(lower, "frame", -1)
    partial_value = add_rims(middle, from_below, from_above, 0)
    lower, middle, upper = split_rims(partial_value, 1)
    from_below = passed_along(upper, "height", 1)
    from_above = passed_along(lower, "height", -1)
    partial_value = add_rims(middle, from_below, from_above, 1)
    lower, middle, upper = split_rims(partial_value, 2)
    from_below = passed_along(upper, "width", 1)
    from_above = passed_along(lower, "width", -1)
    partial_value = add_rims(middle, from_below, from_above, 2)
    key_grad = partial_value[..., :chans].astype(jnp.bfloat16)
    value_grad = partial_value[..., chans:].astype(jnp.bfloat16)
    return (attended, query_grad, key_grad, value_grad)


def solution(mesh):
    return jax.shard_map(
        on_device,
        mesh=mesh,
        in_specs=(
            P("frame", "height", "width", None),
            P("frame", "height", "width", None),
            P("frame", "height", "width", None),
            P("frame", "height", "width", None),
            P(),
        ),
        out_specs=(
            P("frame", "height", "width", None),
            P("frame", "height", "width", None),
            P("frame", "height", "width", None),
            P("frame", "height", "width", None),
        ),
        check_vma=False,
    )
```

profile of v0, /device:TPU:193, one launch (start us, length us, event | category | flops | bytes accessed | tf_op | source)
XLA Modules:
  0.0 599.3 jit_solution(7519256837582965815)
XLA Ops:
  6.2 8.1 %collective-permute-start.1 = (bf16[2,6,6,3072]{3,2,1,0:T(8,128)(2,1)S(1)}, bf16[2,6,6,3072]{3,2,1,0:T(8,128)(2,1)S(1)}, u32[]{:S(2)}, u32[]{:S(2)}) collective-permute-start(bf16[2,6,6,3072]{3,2,1,0:T(8,128)(2,1)S(1)} %get-tuple-element.589), channel_id=1, source_target_pairs={{32,0},{64,32},{96,64},{128,96},{160,128},{192,160},{224,192},{33,... | collective-permute-start | bytes 1327112 | tf_op jit(solution)/shard_map/ppermute | solution.py:21
  14.3 23.6 %collective-permute-done = bf16[2,6,6,3072]{3,2,1,0:T(8,128)(2,1)S(1)} collective-permute-done((bf16[2,6,6,3072]{3,2,1,0:T(8,128)(2,1)S(1)}, bf16[2,6,6,3072]{3,2,1,0:T(8,128)(2,1)S(1)}, u32[]{:S(2)}, u32[]{:S(2)}) %collective-permute-start) | collective-permute-done | bytes 442400 | tf_op jit(solution)/shard_map/ppermute | solution.py:19
  45.4 9.6 %collective-permute-done.3 = bf16[8,2,6,3072]{3,0,2,1:T(8,128)(2,1)S(1)} collective-permute-done((bf16[8,2,6,3072]{3,0,2,1:T(8,128)(2,1)S(1)}, bf16[8,2,6,3072]{3,0,2,1:T(8,128)(2,1)S(1)}, u32[]{:S(2)}, u32[]{:S(2)}) %collective-permute-start.3) | collective-permute-done | bytes 589856 | tf_op jit(solution)/shard_map/ppermute | solution.py:21
  61.3 4.6 collective-permute-start.5
  87.4 6.3 %pad_maximum_fusion = bf16[8,10,10,3072]{3,2,1,0:T(8,128)(2,1)} fusion(bf16[8,10,2,3072]{3,2,1,0:T(2,128)(2,1)S(1)} %copy.75, bf16[8,2,6,3072]{3,2,1,0:T(8,128)(2,1)S(1)} %copy.71, bf16[2,6,6,3072]{3,2,1,0:T(8,128)(2,1)S(1)} %copy-done.2, bf16[4,6,6,3072]{3,2,1,0:T(8,128)(2,1)S(1)} %copy_dynamic-update-slice_fusion, ...), kind=kLoop, calls=%fused_computation.98 | loop fusion | flops 34406400 | bytes 9830400 | tf_op jit(solution)/shard_map/concatenate | solution.py:17
  93.7 9.1 %reshape.135 = bf16[800,3072]{1,0:T(8,128)(2,1)} reshape(bf16[8,10,10,3072]{3,2,1,0:T(8,128)(2,1)} %pad_maximum_fusion) | data formatting | bytes 9830400 | tf_op jit(solution)/shard_map/reshape | solution.py:85
  102.8 4.9 fusion.98
  119.5 108.3 %while.30 = (s32[]{:T(128)}, bf16[12,144,128]{2,1,0:T(8,128)(2,1)S(1)}, f32[12,144]{1,0:T(8,128)S(1)}, s32[12,3]{0,1:T(4,128)S(1)}, bf16[12,144,128]{2,1,0:T(8,1...) while((s32[]{:T(128)}, ...), condition=%wide.region_3.4_spmd.clone.clone, body=%wide.region_0.3_spmd.clone.clone.sunk | while | flops 63136656 | bytes 2047165 | solution.py:103
  121.2 3.5 fusion.126
  148.3 3.5 fusion.126
  230.3 136.0 %while.31 = (s32[]{:T(128)}, bf16[12,144,128]{2,1,0:T(8,128)(2,1)S(1)}, f32[12,800,128]{2,1,0:T(8,128)}, f32[12,800,128]{2,1,0:T(8,128)}, s32[12,3]{0,1:T(4,128)...) while((s32[]{:T(128)}, ...), condition=%wide.region_6.7_spmd.clone.clone, body=%wide.region_5.6_spmd.clone.clone.sunk | while | flops 149997600 | bytes 3826261 | solution.py:141
  366.4 8.1 %copy.93 = f32[800,12,128]{2,1,0:T(8,128)} copy(f32[800,12,128]{2,0,1:T(8,128)} %bitcast.129) | data formatting | bytes 9830400 | tf_op jit(solution)/shard_map/transpose | solution.py:52
  374.5 8.2 %reshape.141 = f32[8,10,10,1536]{3,2,1,0:T(8,128)} reshape(f32[800,12,128]{2,1,0:T(8,128)} %copy.93) | data formatting | bytes 9830400 | tf_op jit(solution)/shard_map/reshape | solution.py:52
  382.7 8.0 %copy.92 = f32[800,12,128]{2,1,0:T(8,128)} copy(f32[800,12,128]{2,0,1:T(8,128)} %bitcast.130) | data formatting | bytes 9830400 | tf_op jit(solution)/shard_map/transpose | solution.py:52
  390.7 8.4 %reshape.140 = f32[8,10,10,1536]{3,2,1,0:T(8,128)} reshape(f32[800,12,128]{2,1,0:T(8,128)} %copy.92) | data formatting | bytes 9830400 | tf_op jit(solution)/shard_map/reshape | solution.py:52
  399.1 4.4 constant_dynamic-update-slice_fusion.1
  403.5 4.3 constant_dynamic-update-slice_fusion
  410.7 10.1 %collective-permute-start.7 = (f32[2,10,10,3072]{3,0,2,1:T(2,128)S(1)}, f32[2,10,10,3072]{3,0,2,1:T(2,128)S(1)}, u32[]{:S(2)}, u32[]{:S(2)}) collective-permute-start(f32[2,10,10,3072]{3,0,2,1:T(2,128)S(1)} %copy.96), channel_id=1, source_target_pairs={{32,0},{64,32},{96,64},{128,96},{160,128},{192,160},{224,192},{33,... | collective-permute-start | bytes 7372808 | tf_op jit(solution)/shard_map/ppermute | solution.py:31
  424.6 100.7 %collective-permute-done.7 = f32[2,10,10,3072]{3,0,2,1:T(2,128)S(1)} collective-permute-done((f32[2,10,10,3072]{3,0,2,1:T(2,128)S(1)}, f32[2,10,10,3072]{3,0,2,1:T(2,128)S(1)}, u32[]{:S(2)}, u32[]{:S(2)}) %collective-permute-start.7) | collective-permute-done | bytes 2457632 | tf_op jit(solution)/shard_map/ppermute | solution.py:31
  528.0 9.2 %collective-permute-done.6 = f32[2,10,10,3072]{3,0,2,1:T(2,128)S(1)} collective-permute-done((f32[2,10,10,3072]{3,0,2,1:T(2,128)S(1)}, f32[2,10,10,3072]{3,0,2,1:T(2,128)S(1)}, u32[]{:S(2)}, u32[]{:S(2)}) %collective-permute-start.6) | collective-permute-done | bytes 2457632 | tf_op jit(solution)/shard_map/ppermute | solution.py:31
  540.0 4.0 fusion.89
  551.1 18.3 %collective-permute-done.9 = f32[4,2,10,3072]{3,0,2,1:T(4,128)S(1)} collective-permute-done((f32[4,2,10,3072]{3,0,2,1:T(4,128)S(1)}, f32[4,2,10,3072]{3,0,2,1:T(4,128)S(1)}, u32[]{:S(2)}, u32[]{:S(2)}) %collective-permute-start.9) | collective-permute-done | bytes 983072 | tf_op jit(solution)/shard_map/ppermute | solution.py:31
  576.0 6.8 %collective-permute-start.10 = (f32[4,6,2,3072]{3,2,1,0:T(2,128)}, f32[4,6,2,3072]{3,2,1,0:T(2,128)S(1)}, u32[]{:S(2)}, u32[]{:S(2)}) collective-permute-start(f32[4,6,2,3072]{3,2,1,0:T(2,128)} %get-tuple-element.580), channel_id=1, source_target_pairs={{0,1},{1,2},{2,3},{3,4},{4,5},{5,6},{6,7},{8,9},{9,10},{10,11},{11... | collective-permute-start | bytes 1769480 | tf_op jit(solution)/shard_map/ppermute | solution.py:31
  590.0 4.4 collective-permute-done.11
  (599 shorter events, 327.5 us)
Async XLA Ops:
  3.0 34.9 %collective-permute-start = (bf16[2,6,6,3072]{3,2,1,0:T(8,128)(2,1)S(1)}, bf16[2,6,6,3072]{3,2,1,0:T(8,128)(2,1)S(1)}, u32[]{:S(2)}, u32[]{:S(2)}) collective-permute-start(bf16[2,6,6,3072]{3,2,1,0:T(8,128)(2,1)S(1)} %get-tuple-element.588), channel_id=1, source_target_pairs={{0,32},{32,64},{64,96},{96,128},{128,160},{160,192},{192,224},{1,3... | collective-permute-start | bytes 1327112 | tf_op jit(solution)/shard_map/ppermute | solution.py:19
  6.2 32.8 %collective-permute-start.1 = (bf16[2,6,6,3072]{3,2,1,0:T(8,128)(2,1)S(1)}, bf16[2,6,6,3072]{3,2,1,0:T(8,128)(2,1)S(1)}, u32[]{:S(2)}, u32[]{:S(2)}) collective-permute-start(bf16[2,6,6,3072]{3,2,1,0:T(8,128)(2,1)S(1)} %get-tuple-element.589), channel_id=1, source_target_pairs={{32,0},{64,32},{96,64},{128,96},{160,128},{192,160},{224,192},{33,... | collective-permute-start | bytes 1327112 | tf_op jit(solution)/shard_map/ppermute | solution.py:21
  39.0 19.0 %copy-start.1 = (bf16[2,6,6,3072]{3,2,1,0:T(8,128)(2,1)}, bf16[2,6,6,3072]{3,2,1,0:T(8,128)(2,1)S(1)}, u32[]{:S(2)}) copy-start(bf16[2,6,6,3072]{3,2,1,0:T(8,128)(2,1)S(1)} %collective-permute-done.1) | copy-start | bytes 1327108
  39.7 15.3 %collective-permute-start.3 = (bf16[8,2,6,3072]{3,0,2,1:T(8,128)(2,1)S(1)}, bf16[8,2,6,3072]{3,0,2,1:T(8,128)(2,1)S(1)}, u32[]{:S(2)}, u32[]{:S(2)}) collective-permute-start(bf16[8,2,6,3072]{3,0,2,1:T(8,128)(2,1)S(1)} %copy.69), channel_id=1, source_target_pairs={{8,0},{16,8},{24,16},{9,1},{17,9},{25,17},{10,2},{18,10},{26,18},{... | collective-permute-start | bytes 1769480 | tf_op jit(solution)/shard_map/ppermute | solution.py:21
  42.7 15.0 %collective-permute-start.2 = (bf16[8,2,6,3072]{3,0,2,1:T(8,128)(2,1)S(1)}, bf16[8,2,6,3072]{3,0,2,1:T(8,128)(2,1)S(1)}, u32[]{:S(2)}, u32[]{:S(2)}) collective-permute-start(bf16[8,2,6,3072]{3,0,2,1:T(8,128)(2,1)S(1)} %copy.68), channel_id=1, source_target_pairs={{0,8},{8,16},{16,24},{1,9},{9,17},{17,25},{2,10},{10,18},{18,26},{... | collective-permute-start | bytes 1769480 | tf_op jit(solution)/shard_map/ppermute | solution.py:19
  61.3 21.7 %collective-permute-start.5 = (bf16[8,10,2,3072]{3,0,2,1:T(8,128)(2,1)}, bf16[8,10,2,3072]{3,0,2,1:T(8,128)(2,1)}, u32[]{:S(2)}, u32[]{:S(2)}) collective-permute-start(bf16[8,10,2,3072]{3,0,2,1:T(8,128)(2,1)} %copy.73), channel_id=1, source_target_pairs={{1,0},{2,1},{3,2},{4,3},{5,4},{6,5},{7,6},{9,8},{10,9},{11,10},{12... | collective-permute-start | bytes 2949128 | tf_op jit(solution)/shard_map/ppermute | solution.py:21
  67.1 18.1 %collective-permute-start.4 = (bf16[8,10,2,3072]{3,0,2,1:T(8,128)(2,1)}, bf16[8,10,2,3072]{3,0,2,1:T(8,128)(2,1)}, u32[]{:S(2)}, u32[]{:S(2)}) collective-permute-start(bf16[8,10,2,3072]{3,0,2,1:T(8,128)(2,1)} %copy.72), channel_id=1, source_target_pairs={{0,1},{1,2},{2,3},{3,4},{4,5},{5,6},{6,7},{8,9},{9,10},{10,11},{11... | collective-permute-start | bytes 2949128 | tf_op jit(solution)/shard_map/ppermute | solution.py:19
  80.9 6.5 %copy-start.2 = (bf16[2,6,6,3072]{3,2,1,0:T(8,128)(2,1)S(1)}, bf16[2,6,6,3072]{3,2,1,0:T(8,128)(2,1)}, u32[]{:S(2)}) copy-start(bf16[2,6,6,3072]{3,2,1,0:T(8,128)(2,1)} %copy-done.1) | copy-start | bytes 1327108
  116.8 2.7 copy-start.4
  119.5 109.0 %copy-start.3 = (bf16[4,6,6,1536]{3,0,2,1:T(4,128)(2,1)S(1)}, bf16[4,6,6,1536]{3,0,2,1:T(4,128)(2,1)}, u32[]{:S(2)}) copy-start(bf16[4,6,6,1536]{3,0,2,1:T(4,128)(2,1)} %param.12) | copy-start | bytes 1327108
  410.7 114.6 %collective-permute-start.7 = (f32[2,10,10,3072]{3,0,2,1:T(2,128)S(1)}, f32[2,10,10,3072]{3,0,2,1:T(2,128)S(1)}, u32[]{:S(2)}, u32[]{:S(2)}) collective-permute-start(f32[2,10,10,3072]{3,0,2,1:T(2,128)S(1)} %copy.96), channel_id=1, source_target_pairs={{32,0},{64,32},{96,64},{128,96},{160,128},{192,160},{224,192},{33,... | collective-permute-start | bytes 7372808 | tf_op jit(solution)/shard_map/ppermute | solution.py:31
  422.7 114.6 %collective-permute-start.6 = (f32[2,10,10,3072]{3,0,2,1:T(2,128)S(1)}, f32[2,10,10,3072]{3,0,2,1:T(2,128)S(1)}, u32[]{:S(2)}, u32[]{:S(2)}) collective-permute-start(f32[2,10,10,3072]{3,0,2,1:T(2,128)S(1)} %copy.94), channel_id=1, source_target_pairs={{0,32},{32,64},{64,96},{96,128},{128,160},{160,192},{192,224},{1,3... | collective-permute-start | bytes 7372808 | tf_op jit(solution)/shard_map/ppermute | solution.py:31
  544.8 24.5 %collective-permute-start.9 = (f32[4,2,10,3072]{3,0,2,1:T(4,128)S(1)}, f32[4,2,10,3072]{3,0,2,1:T(4,128)S(1)}, u32[]{:S(2)}, u32[]{:S(2)}) collective-permute-start(f32[4,2,10,3072]{3,0,2,1:T(4,128)S(1)} %copy.100), channel_id=1, source_target_pairs={{8,0},{16,8},{24,16},{9,1},{17,9},{25,17},{10,2},{18,10},{26,18},{... | collective-permute-start | bytes 2949128 | tf_op jit(solution)/shard_map/ppermute | solution.py:31
  547.7 23.2 %collective-permute-start.8 = (f32[4,2,10,3072]{3,0,2,1:T(4,128)S(1)}, f32[4,2,10,3072]{3,0,2,1:T(4,128)S(1)}, u32[]{:S(2)}, u32[]{:S(2)}) collective-permute-start(f32[4,2,10,3072]{3,0,2,1:T(4,128)S(1)} %copy.98), channel_id=1, source_target_pairs={{0,8},{8,16},{16,24},{1,9},{9,17},{17,25},{2,10},{10,18},{18,26},{... | collective-permute-start | bytes 2949128 | tf_op jit(solution)/shard_map/ppermute | solution.py:31
  572.5 2.1 copy-start
  576.0 13.9 %collective-permute-start.10 = (f32[4,6,2,3072]{3,2,1,0:T(2,128)}, f32[4,6,2,3072]{3,2,1,0:T(2,128)S(1)}, u32[]{:S(2)}, u32[]{:S(2)}) collective-permute-start(f32[4,6,2,3072]{3,2,1,0:T(2,128)} %get-tuple-element.580), channel_id=1, source_target_pairs={{0,1},{1,2},{2,3},{3,4},{4,5},{5,6},{6,7},{8,9},{9,10},{10,11},{11... | collective-permute-start | bytes 1769480 | tf_op jit(solution)/shard_map/ppermute | solution.py:31
  582.8 11.5 %collective-permute-start.11 = (f32[4,6,2,3072]{3,2,1,0:T(2,128)}, f32[4,6,2,3072]{3,2,1,0:T(2,128)}, u32[]{:S(2)}, u32[]{:S(2)}) collective-permute-start(f32[4,6,2,3072]{3,2,1,0:T(2,128)} %get-tuple-element.581), channel_id=1, source_target_pairs={{1,0},{2,1},{3,2},{4,3},{5,4},{6,5},{7,6},{9,8},{10,9},{11,10},{12... | collective-permute-start | bytes 1769480 | tf_op jit(solution)/shard_map/ppermute | solution.py:31
where the time goes:
time: 608 us; the launch traced here: 599 us
  matrix products  198 us (33%)
  waiting for transfers between devices  173 us (28%)
  local copies, waits for them, and re-layouts  154 us (25%)
  starting transfers between devices  50.8 us (8%)
  other arithmetic  20 us (3%)
    ppermute x6, waiting for transfers between devices, passed_along(): return lax.ppermute(block, axis, route)  136 us
    dot_general x36, matrix products, dot_rows(): lax.dot_general(left, right, (((1,), (1,)), ((), ())), preferred_element_...  97.9 us
    dot_general x24, matrix products, dot_cols(): lax.dot_general(left, right, (((0,), (0,)), ((), ())), preferred_element_...  44.7 us
    dot_general x12, matrix products, forward_one_head(): jnp.dot(probs.astype(jnp.bfloat16), value_one, preferred_element_type=jnp...  41.7 us
    ppermute x6, starting transfers between devices, passed_along(): return lax.ppermute(block, axis, route)  26.3 us
    ppermute x3, waiting for transfers between devices, extended(): lax.ppermute(tail, axis, [(i, (i + 1) % count) for i in range(ends)])  25.9 us
    unnamed x23, local copies, waits for them, and re-layouts  25.2 us
    sub x144, local copies, waits for them, and re-layouts, make_mask(): far_axis[None, :] - near_axis[:, None]  16.6 us
  transfers between devices with their start and end apart: 12, of which 10 were waited for; matrix products, arithmetic and copies ran while one was open for 4% of the time, Pallas kernels for 0%

commit v1 on v0

v1 whole, which is shorter than its diff:
```python
import functools

import jax
import jax.numpy as jnp
import numpy as np
from jax import lax
from jax.experimental import pallas as pl
from jax.experimental.pallas import tpu as pltpu
from jax.sharding import PartitionSpec as P

HEADS = 12
HD = 128
EXT = 2
TILE = (4, 6, 6)
CELLS = 144
GROUP = 2
CHUNKS = HEADS // GROUP
HALF = GROUP * HD
LANES = 2 * HALF
SCALE = HD**-0.5
LOG2E = 1.4426950408889634
MESH = pl.DeviceIdType.MESH

FP, FN, HP, HN, WP, WN, PAD, BOX = 144, 224, 304, 400, 496, 672, 848, 896
LAG = (0, 1, 2, 3, 4, 5, 6, 7, 8)
RIM, PIECE, DIRECT = 72, 144, 80
TO_NEXT = ((96, 48, WP), (FP + 48, 32, WP + 48), (FN + 48, 32, WP + 80), (HP + 64, 32, WP + 112), (HN + 64, 32, WP + 144))
TO_PREV = ((0, 48, WN), (FP, 32, WN + 48), (FN, 32, WN + 80), (HP, 32, WN + 112), (HN, 32, WN + 144))


def cell_rows():
    own = [(f, h, w) for w in range(6) for h in range(6) for f in range(4)]
    none = [(99, 99, 99)]
    fp = [(f, h, w) for w in range(6) for h in range(6) for f in (-2, -1)] + none * 8
    fn = [(f, h, w) for w in range(6) for h in range(6) for f in (4, 5)] + none * 8
    hp = [(f, h, w) for w in range(6) for h in (-2, -1) for f in range(-2, 6)]
    hn = [(f, h, w) for w in range(6) for h in (6, 7) for f in range(-2, 6)]
    rows = own + fp + fn + hp + hn
    wp = [(f, h, w - 6) if w in (4, 5) else none[0] for s, n, _ in TO_NEXT for f, h, w in rows[s : s + n]]
    wn = [(f, h, w + 6) if w in (0, 1) else none[0] for s, n, _ in TO_PREV for f, h, w in rows[s : s + n]]
    rows = rows + wp + wn + none * (BOX - PAD)
    return np.array(rows, np.int32)


def tables():
    rows = cell_rows()
    where = {tuple(cell): i for i, cell in enumerate(rows[:HP].tolist()) if cell[0] != 99}
    raw = [(f, h, w) for h in range(6) for w in range(6) for f in range(4)]
    raw_at = {cell: i for i, cell in enumerate(raw)}
    first = np.zeros((CELLS, CELLS), np.float32)
    for i, cell in enumerate(rows[:CELLS].tolist()):
        first[i, raw_at[tuple(cell)]] = 1
    rims = np.zeros((2 * RIM, CELLS), np.float32)
    for i, (f, h, w) in enumerate(rows[FN : FN + RIM].tolist()):
        rims[i, raw_at[(f - 4, h, w)]] = 1
    for i, (f, h, w) in enumerate(rows[FP : FP + RIM].tolist()):
        rims[RIM + i, raw_at[(f + 4, h, w)]] = 1
    packed = np.zeros((2 * PIECE, 2 * CELLS), np.float32)
    for s in range(2):
        packed[s * PIECE : s * PIECE + RIM, :CELLS] = rims[s * RIM : s * RIM + RIM]
        packed[s * PIECE + RIM : s * PIECE + PIECE, CELLS:] = rims[s * RIM : s * RIM + RIM]
    second = np.zeros((192, HP), np.float32)
    for i, (f, h, w) in enumerate(rows[HN : HN + 96].tolist()):
        second[i, where[(f, h - 6, w)]] = 1
    for i, (f, h, w) in enumerate(rows[HP : HP + 96].tolist()):
        second[96 + i, where[(f, h + 6, w)]] = 1
    code = np.full((CELLS, BOX), 255, np.int32)
    for axis, (one, two) in enumerate(((0x0F, 0xF0), (0x33, 0xCC), (0x55, 0xAA))):
        gap = np.abs(np.array(raw)[:, None, axis] - rows[None, :, axis])
        code &= np.where(gap <= 1, one, 0) | np.where(gap <= 2, two, 0)
    side = np.zeros((8, BOX), np.int32)
    for axis, size in enumerate(TILE):
        side |= np.where(rows[:, axis] < 0, 1 << (2 * axis), 0)[None].astype(np.int32)
        side |= np.where(rows[:, axis] >= size, 2 << (2 * axis), 0)[None].astype(np.int32)
    frames = first @ rims.T
    as_bf16 = [array.astype(jnp.bfloat16) for array in (first, packed, second, second.T, frames, first.T)]
    return (*as_bf16, code, side)


def dot(left, right, sides=((1,), (0,))):
    return lax.dot_general(left, right, (sides, ((), ())), preferred_element_type=jnp.float32)


def kernel(
    ext,
    q_ref,
    k_ref,
    v_ref,
    d_ref,
    first_ref,
    packed_ref,
    second_ref,
    second_t_ref,
    frames_ref,
    order_ref,
    code_ref,
    side_ref,
    att_out,
    dq_out,
    dk_out,
    dv_out,
    box,
    f_send,
    f_in,
    h_send,
    w_send,
    w_back,
    h_back,
    f_back,
    w_got,
    h_got,
    f_got,
    by_way,
    acc,
    send_sem,
    recv_sem,
):
    axes = ("frame", "height", "width")
    index = [lax.axis_index(axis) for axis in axes]
    has_prev = [i > 0 for i in index]
    has_next = [i < lax.axis_size(axis) - 1 for i, axis in zip(index, axes)]
    sides = []
    for axis in range(3):
        sides.append((2 * axis, axes[axis], index[axis] - 1, has_prev[axis]))
        sides.append((2 * axis + 1, axes[axis], index[axis] + 1, has_next[axis]))

    frame, frames = index[0], lax.axis_size("frame")
    shared = frames == 8
    low_mid, high_mid = frames // 2 - 1, frames // 2
    crossing = [(frame == high_mid), (frame == low_mid)] if shared else [False, False]

    def copy(src, dst, number, number_there, axis, other, c):
        return pltpu.make_async_remote_copy(
            src_ref=src,
            dst_ref=dst,
            send_sem=send_sem.at[number, c],
            recv_sem=recv_sem.at[number_there, c],
            device_id={axis: other},
            device_id_type=MESH,
        )

    def remote(src, dst, number, s, c):
        _, axis, other, _ = sides[s]
        return copy(src, dst, number, number, axis, other, c)

    box[:, PAD:BOX, :] = jnp.zeros((CHUNKS, BOX - PAD, LANES), jnp.bfloat16)
    backs = ((h_back, h_got, 96), (w_back, w_got, 176))
    regions = ((FP, FN), (FN, HP), (HP, HN), (HN, WP), (WP, WN), (WN, PAD))
    for (number, _, _, present), (low, high) in zip(sides, regions):

        @pl.when(jnp.logical_not(present))
        def _(number=number, low=low, high=high):
            if number < 2:
                at = PIECE * number
                for got in (f_in, f_got):
                    got[:, at : at + PIECE, :] = jnp.zeros((CHUNKS, PIECE, HALF), jnp.bfloat16)
            else:
                box[:, low:high, :] = jnp.zeros((CHUNKS, high - low, LANES), jnp.bfloat16)
            if number in (2, 3):
                at = 96 * (number - 2)
                h_got[:, at : at + 96, :] = jnp.zeros((CHUNKS, 96, LANES), jnp.bfloat16)

    barrier = pltpu.get_barrier_semaphore()
    for _, axis, other, present in sides:

        @pl.when(present)
        def _(axis=axis, other=other):
            pl.semaphore_signal(barrier, inc=1, device_id={axis: other}, device_id_type=MESH)

    greeted = sum(jnp.where(present, 1, 0) for _, _, _, present in sides)
    if shared:
        for here, others in ((0, (low_mid, high_mid)), (low_mid, (0, frames - 1)), (high_mid, (0, frames - 1)), (frames - 1, (low_mid, high_mid))):

            @pl.when(frame == here)
            def _(others=others):
                for other in others:
                    pl.semaphore_signal(barrier, inc=1, device_id={"frame": other}, device_id_type=MESH)

            greeted = greeted + jnp.where(frame == here, 2, 0)
    pl.semaphore_wait(barrier, greeted)

    def frame_copies(way, s, c, act):
        src, dst = ((f_send, f_in), (f_back, f_got))[way]
        here, there, number = PIECE * s, PIECE * (1 - s), 6 * way + (s ^ 1)
        if not shared:
            act(remote(src.at[c, pl.ds(here, PIECE)], dst.at[c, pl.ds(there, PIECE)], number, s, c))
            return

        @pl.when(jnp.logical_not(crossing[s]))
        def _():
            act(remote(src.at[c, pl.ds(here, PIECE)], dst.at[c, pl.ds(there, PIECE)], number, s, c))

        @pl.when(crossing[s])
        def _():
            rest = src.at[c, pl.ds(here + DIRECT, PIECE - DIRECT)]
            act(copy(rest, by_way.at[way, c], 12 + way, 12 + way, "frame", (0, frames - 1)[s], c))
            act(remote(src.at[c, pl.ds(here, DIRECT)], dst.at[c, pl.ds(there, DIRECT)], number, s, c))

    def forward(way, c, act):
        for s, here, there in ((1, 0, low_mid), (0, frames - 1, high_mid)):

            @pl.when(frame == here)
            def _(s=s, there=there):
                dst = (f_in, f_got)[way].at[c, pl.ds(PIECE * s + DIRECT, PIECE - DIRECT)]
                act(copy(by_way.at[way, c], dst, 14 + way, 6 * way + s, "frame", there, c))

    def step_forward(way, c):
        if shared:

            @pl.when((frame == 0) | (frame == frames - 1))
            def _():
                held = by_way.at[way, c]
                copy(held, held, 12 + way, 12 + way, "frame", jnp.where(frame == 0, high_mid, low_mid), c).wait_recv()

            forward(way, c, lambda copy: copy.start())

    def frames_come(way, s, c):
        got = (f_in, f_got)[way].at[c, pl.ds(PIECE * s, PIECE)]
        remote(got, got, 6 * way + s, s, c).wait_recv()

    def height_copy(s, c):
        src = h_send.at[c, pl.ds(96 * (s - 2), 96)]
        return remote(src, box.at[c, pl.ds((HN, HP)[s - 2], 96)], s ^ 1, s, c)

    def width_copy(s, c):
        src = w_send.at[c, pl.ds(176 * (s - 4), 176)]
        return remote(src, box.at[c, pl.ds((WN, WP)[s - 4], 176)], s ^ 1, s, c)

    def back_copy(s, c):
        src, dst, rows = backs[s // 2 - 1]
        low = rows * (s % 2)
        return remote(src.at[c, pl.ds(low, rows)], dst.at[c, pl.ds(rows - low, rows)], 6 + (s ^ 1), s, c)

    def region(s, c):
        return box.at[c, pl.ds(regions[s][0], regions[s][1] - regions[s][0])]

    def come(s, c):
        remote(region(s, c), region(s, c), s, s, c).wait_recv()

    def come_back(s, c):
        _, dst, rows = backs[s // 2 - 1]
        got = dst.at[c, pl.ds(rows * (s % 2), rows)]
        remote(got, got, 6 + s, s, c).wait_recv()

    def all_sent(s, c):
        if s < 2:
            for way in (0, 1):
                frame_copies(way, s, c, lambda copy: copy.wait_send())
        else:
            remote(region(s, c), region(s, c), s ^ 1, s, c).wait_send()
            back_copy(s, c).wait_send()

    def on_sides(group, act):
        for s in group:
            pl.when(sides[s][3])(functools.partial(act, s))

    def lanes_of(c, count):
        return pl.ds(pl.multiple_of(c * count * HD, count * HD), count * HD)

    def load(ref, c, count=1):
        return ref[:, :, lanes_of(c, count)].reshape(CELLS, count * HD)

    def store(ref, c, value, count=1):
        ref[:, :, lanes_of(c, count)] = value.astype(jnp.bfloat16).reshape(CELLS // 4, 4, count * HD)

    def step_first(c):
        key, value = load(k_ref, c, GROUP), load(v_ref, c, GROUP)
        f_send[c] = dot(packed_ref[...], jnp.concatenate([key, value], axis=0)).astype(jnp.bfloat16)
        on_sides((0, 1), lambda s: frame_copies(0, s, c, lambda copy: copy.start()))
        both = jnp.concatenate([key, value], axis=1)
        box[c, 0:CELLS, :] = dot(first_ref[...], both).astype(jnp.bfloat16)

    def step_frames(c):
        on_sides((0, 1), lambda s: frames_come(0, s, c))
        got = f_in[c].astype(jnp.float32)
        pad = jnp.zeros((FN - FP - RIM, HALF), jnp.float32)
        for half in (0, 1):
            low = RIM * half
            rims = [got[low : low + RIM], pad, got[PIECE + low : PIECE + low + RIM], pad]
            box[c, FP:HP, HALF * half : HALF * half + HALF] = jnp.concatenate(rims, axis=0).astype(jnp.bfloat16)
        h_send[c] = dot(second_ref[...], box[c, 0:HP, :]).astype(jnp.bfloat16)
        on_sides((2, 3), lambda s: height_copy(s, c).start())

    def step_rows(c):
        on_sides((2, 3), lambda s: come(s, c))
        for s in (4, 5):
            for start, count, there in (TO_PREV, TO_NEXT)[s - 4]:
                at = there - (WN, WP)[s - 4] + 176 * (s - 4)
                w_send[c, at : at + count, :] = box[c, start : start + count, :]
        on_sides((4, 5), lambda s: width_copy(s, c).start())

    def step_attend(c):
        on_sides((4, 5), lambda s: come(s, c))
        edges = sum(jnp.where(present, 0, 1 << number) for number, _, _, present in sides)
        open_side = (side_ref[0:1, :] & edges) == 0
        for g in range(GROUP):
            head = c * GROUP + g
            key_lanes = slice(g * HD, g * HD + HD)
            value_lanes = slice(HALF + g * HD, HALF + g * HD + HD)
            kind = (15 * ext[0, head] - 14) * (3 * ext[1, head] - 2) * ext[2, head]
            kinds = jnp.where(open_side, kind, 0)
            query, grad = load(q_ref, head), load(d_ref, head)
            key, value = box[c, :, key_lanes], box[c, :, value_lanes]
            scores = dot(query, key, ((1,), (1,)))
            scores = jnp.where((code_ref[...] & kinds) != 0, scores, -1e30)
            top = jnp.max(scores, axis=1, keepdims=True)
            raised = jnp.exp2((scores - top) * (SCALE * LOG2E))
            probs = raised * (1.0 / jnp.sum(raised, axis=1, keepdims=True))
            weights = probs.astype(jnp.bfloat16)
            attended = dot(weights, value).astype(jnp.bfloat16)
            store(att_out, head, attended)
            delta = jnp.sum(grad.astype(jnp.float32) * attended.astype(jnp.float32), axis=1, keepdims=True)
            dprobs = dot(grad, value, ((1,), (1,)))
            dscores = (probs * (dprobs - delta) * SCALE).astype(jnp.bfloat16)
            store(dq_out, head, dot(dscores, key))
            key_part = dot(dscores, query, ((0,), (0,)))
            value_part = dot(weights, grad, ((0,), (0,)))
            for part, lanes in ((key_part, key_lanes), (value_part, value_lanes)):
                acc[c, :, lanes] = part[0:WP]
                w_back[c, :, lanes] = part[WP:PAD].astype(jnp.bfloat16)
        on_sides((4, 5), lambda s: back_copy(s, c).start())

    def step_back_columns(c):
        def take(s):
            come_back(s, c)
            for start, count, there in (TO_PREV, TO_NEXT)[s - 4]:
                low = there - (WN, WP)[s - 4] + 176 * (s - 4)
                acc[c, start : start + count, :] += w_got[c, low : low + count, :].astype(jnp.float32)

        on_sides((4, 5), take)
        h_back[c] = acc[c, HP:WP, :].astype(jnp.bfloat16)
        on_sides((2, 3), lambda s: back_copy(s, c).start())

    def step_back_rows(c):
        on_sides((2, 3), lambda s: come_back(s, c))
        acc[c, 0:HP, :] += dot(second_t_ref[...], h_got[c])
        rims = [acc[c, low : low + RIM, HALF * half : HALF * half + HALF] for low in (FP, FN) for half in (0, 1)]
        f_back[c] = jnp.concatenate(rims, axis=0).astype(jnp.bfloat16)
        on_sides((0, 1), lambda s: frame_copies(1, s, c, lambda copy: copy.start()))

    def step_back_frames(c):
        on_sides((0, 1), lambda s: frames_come(1, s, c))
        got = f_got[c].astype(jnp.float32)
        halves = [jnp.concatenate([got[low : low + RIM], got[PIECE + low : PIECE + low + RIM]], axis=0) for low in (0, RIM)]
        terms = jnp.concatenate(halves, axis=1).astype(jnp.bfloat16)
        total = (acc[c, 0:CELLS, :] + dot(frames_ref[...], terms)).astype(jnp.bfloat16)
        total = dot(order_ref[...], total)
        store(dk_out, c, total[:, 0:HALF], GROUP)
        store(dv_out, c, total[:, HALF:LANES], GROUP)

    def tick(t, carry):
        for step, lag in zip(
            (
                step_first,
                functools.partial(step_forward, 0),
                step_frames,
                step_rows,
                step_attend,
                step_back_columns,
                step_back_rows,
                functools.partial(step_forward, 1),
                step_back_frames,
            ),
            LAG,
        ):
            c = t - lag
            pl.when((c >= 0) & (c < CHUNKS))(functools.partial(step, c))
        return carry

    lax.fori_loop(0, CHUNKS + LAG[-1], tick, 0)

    def finish(c, carry):
        on_sides(range(6), lambda s: all_sent(s, c))
        if shared:
            for way in (0, 1):
                forward(way, c, lambda copy: copy.wait_send())
        return carry

    lax.fori_loop(0, CHUNKS, finish, 0)


def hand_out(*refs):
    for i in range(4):
        refs[4 + i][...] = refs[i][...]


def on_device(queries, keys, values, out_grad, extents):
    flat = [array.transpose(1, 2, 0, 3).reshape(36, 4, HEADS * HD) for array in (queries, keys, values, out_grad)]
    shape = jax.ShapeDtypeStruct((36, 4, HEADS * HD), jnp.bfloat16)
    vmem = pl.BlockSpec(memory_space=pltpu.VMEM)
    wide, narrow = LANES, HALF
    held = [(BOX, wide), (288, narrow), (288, narrow), (192, wide), (352, wide), (352, wide), (192, wide), (288, narrow)]
    held += [(352, wide), (192, wide), (288, narrow)]
    results = pl.pallas_call(
        kernel,
        out_shape=(shape,) * 4,
        in_specs=[pl.BlockSpec(memory_space=pltpu.SMEM)] + [vmem] * 12,
        out_specs=(vmem,) * 4,
        scratch_shapes=[pltpu.VMEM((CHUNKS, *dims), jnp.bfloat16) for dims in held]
        + [
            pltpu.VMEM((2, CHUNKS, PIECE - DIRECT, HALF), jnp.bfloat16),
            pltpu.VMEM((CHUNKS, WP, LANES), jnp.float32),
            pltpu.SemaphoreType.DMA((16, CHUNKS)),
            pltpu.SemaphoreType.DMA((14, CHUNKS)),
        ],
        compiler_params=pltpu.CompilerParams(
            collective_id=0, has_side_effects=True, vmem_limit_bytes=42 * 1024 * 1024
        ),
        cost_estimate=pl.CostEstimate(flops=2_500_000_000, bytes_accessed=8_000_000, transcendentals=1_500_000),
    )(extents.T, *flat, *[jnp.asarray(table) for table in tables()])
    results = pl.pallas_call(
        hand_out,
        out_shape=(shape,) * 4,
        in_specs=[vmem] * 4,
        out_specs=(vmem,) * 4,
        cost_estimate=pl.CostEstimate(flops=0, bytes_accessed=3_600_000, transcendentals=0),
    )(*results)
    return tuple(result.reshape(6, 6, 4, HEADS * HD).transpose(2, 0, 1, 3) for result in results)


def solution(mesh):
    spec = P("frame", "height", "width", None)
    return jax.shard_map(
        on_device,
        mesh=mesh,
        in_specs=(spec, spec, spec, spec, P()),
        out_specs=(spec, spec, spec, spec),
        check_vma=False,
    )
```

time: 608 us -> 100 us (0.16)
  the two profiles are of different devices: /device:TPU:193 before, /device:TPU:26 now
where the time goes in v1:
time: 100 us; the launch traced here: 99.6 us
  Pallas kernels  84.8 us (85%)
  local copies, waits for them, and re-layouts  14.1 us (14%)
    pallas_call x1, Pallas kernels, on_device(): pl.pallas_call(kernel, out_shape=(shape,) * 4, in_specs=[pl.BlockSpec(mem...  82.2 us
    unnamed x32, local copies, waits for them, and re-layouts  14.1 us
    pallas_call x1, Pallas kernels, on_device(): pl.pallas_call(hand_out, out_shape=(shape,) * 4, in_specs=[vmem] * 4, out...  2.64 us

profile of v1, /device:TPU:26, one launch (start us, length us, event | category | flops | bytes accessed | tf_op | source)
XLA Modules:
  0.0 99.6 jit_solution(13175495762575315916)
XLA Ops:
  0.6 0.0 copy-start.8
  0.6 0.7 copy-done.8
  1.3 0.0 copy-start.4
  1.3 1.0 %copy-done.4 = bf16[4,6,6,1536]{3,0,2,1:T(4,128)(2,1)S(1)} copy-done((bf16[4,6,6,1536]{3,0,2,1:T(4,128)(2,1)S(1)}, bf16[4,6,6,1536]{3,0,2,1:T(4,128)(2,1)}, u32[]{:S(2)}) %copy-start.4) | copy-done | bytes 442392
  2.3 0.0 copy-start.5
  2.3 1.0 %copy-done.5 = bf16[4,6,6,1536]{3,0,2,1:T(4,128)(2,1)S(1)} copy-done((bf16[4,6,6,1536]{3,0,2,1:T(4,128)(2,1)S(1)}, bf16[4,6,6,1536]{3,0,2,1:T(4,128)(2,1)}, u32[]{:S(2)}) %copy-start.5) | copy-done | bytes 442392
  3.3 0.0 copy-start.6
  3.3 1.0 %copy-done.6 = bf16[4,6,6,1536]{3,0,2,1:T(4,128)(2,1)S(1)} copy-done((bf16[4,6,6,1536]{3,0,2,1:T(4,128)(2,1)S(1)}, bf16[4,6,6,1536]{3,0,2,1:T(4,128)(2,1)}, u32[]{:S(2)}) %copy-start.6) | copy-done | bytes 442392
  4.4 0.0 copy-start.7
  4.4 1.0 %copy-done.7 = bf16[4,6,6,1536]{3,0,2,1:T(4,128)(2,1)S(1)} copy-done((bf16[4,6,6,1536]{3,0,2,1:T(4,128)(2,1)S(1)}, bf16[4,6,6,1536]{3,0,2,1:T(4,128)(2,1)}, u32[]{:S(2)}) %copy-start.7) | copy-done | bytes 442392
  5.4 1.0 %copy-done.9 = s32[144,896]{1,0:T(8,128)S(1)} copy-done((s32[144,896]{1,0:T(8,128)S(1)}, s32[144,896]{1,0:T(8,128)}, u32[]{:S(2)}) %copy-start.9) | copy-done | bytes 516120
  6.4 0.9 copy-done.10
  7.3 0.9 copy-done.11
  8.3 0.9 copy-done.12
  9.2 0.9 copy-done.13
  10.1 0.9 copy-done.14
  10.9 0.7 copy-done.15
  11.7 82.2 %shard_map.156 = (bf16[36,4,1536]{2,1,0:T(4,128)(2,1)S(1)}, bf16[36,4,1536]{2,1,0:T(4,128)(2,1)S(1)}, bf16[36,4,1536]{2,1,0:T(4,128)(2,1)S(1)}, bf16[36,4,1536]{2,1,0:T(4,128)(2,1)S(1)}) custom-call(s32[3,12]{1,0:T(4,128)S(1)} %bitcast.29, bf16[36,4,1536]{2,1,0:T(4,128)(2,1)S(1)} %bitcast.25, bf16[36,4,1536]{2,1,0:T(4,128)(2,1)S(1)} %bitcast.26, ...), custom_call_target="tpu_custom_call" | custom-call | flops 2500000000 | bytes 8000000 | tf_op jit(solution)/shard_map/pallas_call | solution.py:394
  93.9 0.0 copy-start
  93.9 0.8 copy-done
  94.7 0.8 copy-done.1
  95.4 0.8 copy-done.2
  96.2 0.8 copy-done.3
  97.0 2.6 %shard_map.157 = (bf16[36,4,1536]{2,1,0:T(4,128)(2,1)}, bf16[36,4,1536]{2,1,0:T(4,128)(2,1)}, bf16[36,4,1536]{2,1,0:T(4,128)(2,1)}, bf16[36,4,1536]{2,1,0:T(4,128)(2,1)}) custom-call(bf16[36,4,1536]{2,1,0:T(4,128)(2,1)} %copy-done, bf16[36,4,1536]{2,1,0:T(4,128)(2,1)} %copy-done.1, bf16[36,4,1536]{2,1,0:T(4,128)(2,1)} %copy-done.2, ...), custom_call_target="tpu_custom_call" | custom-call | bytes 3600000 | tf_op jit(solution)/shard_map/pallas_call | solution.py:411
  (10 shorter events, 0.0 us)
Async XLA Ops:
  0.6 0.7 copy-start.8
  1.3 1.0 %copy-start.4 = (bf16[4,6,6,1536]{3,0,2,1:T(4,128)(2,1)S(1)}, bf16[4,6,6,1536]{3,0,2,1:T(4,128)(2,1)}, u32[]{:S(2)}) copy-start(bf16[4,6,6,1536]{3,0,2,1:T(4,128)(2,1)} %param.13) | copy-start | bytes 1327108
  2.3 1.0 %copy-start.5 = (bf16[4,6,6,1536]{3,0,2,1:T(4,128)(2,1)S(1)}, bf16[4,6,6,1536]{3,0,2,1:T(4,128)(2,1)}, u32[]{:S(2)}) copy-start(bf16[4,6,6,1536]{3,0,2,1:T(4,128)(2,1)} %param.14) | copy-start | bytes 1327108
  3.3 1.0 %copy-start.6 = (bf16[4,6,6,1536]{3,0,2,1:T(4,128)(2,1)S(1)}, bf16[4,6,6,1536]{3,0,2,1:T(4,128)(2,1)}, u32[]{:S(2)}) copy-start(bf16[4,6,6,1536]{3,0,2,1:T(4,128)(2,1)} %param.15) | copy-start | bytes 1327108
  4.4 1.0 %copy-start.7 = (bf16[4,6,6,1536]{3,0,2,1:T(4,128)(2,1)S(1)}, bf16[4,6,6,1536]{3,0,2,1:T(4,128)(2,1)}, u32[]{:S(2)}) copy-start(bf16[4,6,6,1536]{3,0,2,1:T(4,128)(2,1)} %param.16) | copy-start | bytes 1327108
  5.4 1.0 %copy-start.9 = (s32[144,896]{1,0:T(8,128)S(1)}, s32[144,896]{1,0:T(8,128)}, u32[]{:S(2)}) copy-start(s32[144,896]{1,0:T(8,128)} %constant.19.clone.code_ref) | copy-start | bytes 1548292
  6.4 0.9 copy-start.10
  7.3 0.9 copy-start.11
  8.3 0.9 copy-start.12
  9.2 0.9 copy-start.13
  10.1 0.9 copy-start.14
  10.9 0.7 copy-start.15
  93.9 0.8 copy-start
  94.7 0.8 copy-start.1
  95.4 0.8 copy-start.2
  96.2 0.8 copy-start.3

commit v2 on v1

--- a/solution.py
+++ b/solution.py
@@ -23,7 +23,7 @@
 
 FP, FN, HP, HN, WP, WN, PAD, BOX = 144, 224, 304, 400, 496, 672, 848, 896
 LAG = (0, 1, 2, 3, 4, 5, 6, 7, 8)
-RIM, PIECE, DIRECT = 72, 144, 80
+RIM, PIECE, DIRECT, RELAYED = 72, 144, 48, 32
 TO_NEXT = ((96, 48, WP), (FP + 48, 32, WP + 48), (FN + 48, 32, WP + 80), (HP + 64, 32, WP + 112), (HN + 64, 32, WP + 144))
 TO_PREV = ((0, 48, WN), (FP, 32, WN + 48), (FN, 32, WN + 80), (HP, 32, WN + 112), (HN, 32, WN + 144))
 
@@ -45,16 +45,11 @@
 def tables():
     rows = cell_rows()
     where = {tuple(cell): i for i, cell in enumerate(rows[:HP].tolist()) if cell[0] != 99}
-    raw = [(f, h, w) for h in range(6) for w in range(6) for f in range(4)]
-    raw_at = {cell: i for i, cell in enumerate(raw)}
-    first = np.zeros((CELLS, CELLS), np.float32)
-    for i, cell in enumerate(rows[:CELLS].tolist()):
-        first[i, raw_at[tuple(cell)]] = 1
     rims = np.zeros((2 * RIM, CELLS), np.float32)
     for i, (f, h, w) in enumerate(rows[FN : FN + RIM].tolist()):
-        rims[i, raw_at[(f - 4, h, w)]] = 1
+        rims[i, where[(f - 4, h, w)]] = 1
     for i, (f, h, w) in enumerate(rows[FP : FP + RIM].tolist()):
-        rims[RIM + i, raw_at[(f + 4, h, w)]] = 1
+        rims[RIM + i, where[(f + 4, h, w)]] = 1
     packed = np.zeros((2 * PIECE, 2 * CELLS), np.float32)
     for s in range(2):
         packed[s * PIECE : s * PIECE + RIM, :CELLS] = rims[s * RIM : s * RIM + RIM]
@@ -66,14 +61,13 @@
         second[96 + i, where[(f, h + 6, w)]] = 1
     code = np.full((CELLS, BOX), 255, np.int32)
     for axis, (one, two) in enumerate(((0x0F, 0xF0), (0x33, 0xCC), (0x55, 0xAA))):
-        gap = np.abs(np.array(raw)[:, None, axis] - rows[None, :, axis])
+        gap = np.abs(rows[:CELLS, None, axis] - rows[None, :, axis])
         code &= np.where(gap <= 1, one, 0) | np.where(gap <= 2, two, 0)
     side = np.zeros((8, BOX), np.int32)
     for axis, size in enumerate(TILE):
         side |= np.where(rows[:, axis] < 0, 1 << (2 * axis), 0)[None].astype(np.int32)
         side |= np.where(rows[:, axis] >= size, 2 << (2 * axis), 0)[None].astype(np.int32)
-    frames = first @ rims.T
-    as_bf16 = [array.astype(jnp.bfloat16) for array in (first, packed, second, second.T, frames, first.T)]
+    as_bf16 = [array.astype(jnp.bfloat16) for array in (packed, second, second.T, rims.T)]
     return (*as_bf16, code, side)
 
 
@@ -87,12 +81,10 @@
     k_ref,
     v_ref,
     d_ref,
-    first_ref,
     packed_ref,
     second_ref,
     second_t_ref,
     frames_ref,
-    order_ref,
     code_ref,
     side_ref,
     att_out,
@@ -112,6 +104,7 @@
     f_got,
     by_way,
     acc,
+    rows_ref,
     send_sem,
     recv_sem,
 ):
@@ -128,6 +121,7 @@
     shared = frames == 8
     low_mid, high_mid = frames // 2 - 1, frames // 2
     crossing = [(frame == high_mid), (frame == low_mid)] if shared else [False, False]
+    helpers = (range(low_mid), range(high_mid + 1, frames))
 
     def copy(src, dst, number, number_there, axis, other, c):
         return pltpu.make_async_remote_copy(
@@ -169,14 +163,16 @@
 
     greeted = sum(jnp.where(present, 1, 0) for _, _, _, present in sides)
     if shared:
-        for here, others in ((0, (low_mid, high_mid)), (low_mid, (0, frames - 1)), (high_mid, (0, frames - 1)), (frames - 1, (low_mid, high_mid))):
+        middle, rest = (low_mid, high_mid), [*helpers[0], *helpers[1]]
+        for here in range(frames):
+            others = [other for other in (rest if here in middle else middle) if abs(other - here) > 1]
 
             @pl.when(frame == here)
             def _(others=others):
                 for other in others:
                     pl.semaphore_signal(barrier, inc=1, device_id={"frame": other}, device_id_type=MESH)
 
-            greeted = greeted + jnp.where(frame == here, 2, 0)
+            greeted = greeted + jnp.where(frame == here, len(others), 0)
     pl.semaphore_wait(barrier, greeted)
 
     def frame_copies(way, s, c, act):
@@ -192,25 +188,29 @@
 
         @pl.when(crossing[s])
         def _():
-            rest = src.at[c, pl.ds(here + DIRECT, PIECE - DIRECT)]
-            act(copy(rest, by_way.at[way, c], 12 + way, 12 + way, "frame", (0, frames - 1)[s], c))
+            for i, helper in enumerate(helpers[s]):
+                part = src.at[c, pl.ds(here + DIRECT + RELAYED * i, RELAYED)]
+                act(copy(part, by_way.at[way, c], 12 + 4 * way + i, 12 + way, "frame", helper, c))
             act(remote(src.at[c, pl.ds(here, DIRECT)], dst.at[c, pl.ds(there, DIRECT)], number, s, c))
 
     def forward(way, c, act):
-        for s, here, there in ((1, 0, low_mid), (0, frames - 1, high_mid)):
-
-            @pl.when(frame == here)
-            def _(s=s, there=there):
-                dst = (f_in, f_got)[way].at[c, pl.ds(PIECE * s + DIRECT, PIECE - DIRECT)]
-                act(copy(by_way.at[way, c], dst, 14 + way, 6 * way + s, "frame", there, c))
+        for s, there in ((1, low_mid), (0, high_mid)):
+            for i, helper in enumerate(helpers[1 - s]):
+
+                @pl.when(frame == helper)
+                def _(s=s, there=there, i=i):
+                    rows = pl.ds(PIECE * s + DIRECT + RELAYED * i, RELAYED)
+                    dst = (f_in, f_got)[way].at[c, rows]
+                    act(copy(by_way.at[way, c], dst, 15 + 4 * way, 6 * way + s, "frame", there, c))
 
     def step_forward(way, c):
         if shared:
 
-            @pl.when((frame == 0) | (frame == frames - 1))
+            @pl.when((frame < low_mid) | (frame > high_mid))
             def _():
                 held = by_way.at[way, c]
-                copy(held, held, 12 + way, 12 + way, "frame", jnp.where(frame == 0, high_mid, low_mid), c).wait_recv()
+                come_from = jnp.where(frame < low_mid, high_mid, low_mid)
+                copy(held, held, 12 + way, 12 + way, "frame", come_from, c).wait_recv()
 
             forward(way, c, lambda copy: copy.start())
 
@@ -254,21 +254,41 @@
         for s in group:
             pl.when(sides[s][3])(functools.partial(act, s))
 
-    def lanes_of(c, count):
-        return pl.ds(pl.multiple_of(c * count * HD, count * HD), count * HD)
-
-    def load(ref, c, count=1):
-        return ref[:, :, lanes_of(c, count)].reshape(CELLS, count * HD)
-
-    def store(ref, c, value, count=1):
-        ref[:, :, lanes_of(c, count)] = value.astype(jnp.bfloat16).reshape(CELLS // 4, 4, count * HD)
+    def regroup(act):
+        def column(w, carry):
+            for h in (0, 2, 4):
+                act((h * 6 + w, h * 6 + 6 + w), pl.ds(pl.multiple_of(w * 24 + 4 * h, 8), 8))
+            return carry
+
+        lax.fori_loop(0, 6, column, 0)
+
+    def lanes_of(c):
+        return pl.ds(pl.multiple_of(c * HALF, HALF), HALF)
+
+    def load(refs, slot, c):
+        def act(places, rows):
+            for n, ref in enumerate(refs):
+                pair = [ref[place, :, lanes_of(c)].astype(jnp.float32) for place in places]
+                rows_ref[slot + n, rows, :] = jnp.concatenate(pair, axis=0)
+
+        regroup(act)
+        return [rows_ref[slot + n].astype(jnp.bfloat16) for n in range(len(refs))]
+
+    def store(refs, slot, c):
+        def act(places, rows):
+            for n, ref in enumerate(refs):
+                pair = rows_ref[slot + n, rows, :]
+                for k, place in enumerate(places):
+                    ref[place, :, lanes_of(c)] = pair[4 * k : 4 * k + 4].astype(jnp.bfloat16)
+
+        regroup(act)
 
     def step_first(c):
-        key, value = load(k_ref, c, GROUP), load(v_ref, c, GROUP)
+        key, value = load((k_ref, v_ref), 0, c)
         f_send[c] = dot(packed_ref[...], jnp.concatenate([key, value], axis=0)).astype(jnp.bfloat16)
         on_sides((0, 1), lambda s: frame_copies(0, s, c, lambda copy: copy.start()))
-        both = jnp.concatenate([key, value], axis=1)
-        box[c, 0:CELLS, :] = dot(first_ref[...], both).astype(jnp.bfloat16)
+        box[c, 0:CELLS, 0:HALF] = key
+        box[c, 0:CELLS, HALF:LANES] = value
 
     def step_frames(c):
         on_sides((0, 1), lambda s: frames_come(0, s, c))
@@ -293,13 +313,14 @@
         on_sides((4, 5), lambda s: come(s, c))
         edges = sum(jnp.where(present, 0, 1 << number) for number, _, _, present in sides)
         open_side = (side_ref[0:1, :] & edges) == 0
+        queries, grads = load((q_ref, d_ref), 2, c)
         for g in range(GROUP):
             head = c * GROUP + g
             key_lanes = slice(g * HD, g * HD + HD)
             value_lanes = slice(HALF + g * HD, HALF + g * HD + HD)
             kind = (15 * ext[0, head] - 14) * (3 * ext[1, head] - 2) * ext[2, head]
             kinds = jnp.where(open_side, kind, 0)
-            query, grad = load(q_ref, head), load(d_ref, head)
+            query, grad = queries[:, key_lanes], grads[:, key_lanes]
             key, value = box[c, :, key_lanes], box[c, :, value_lanes]
             scores = dot(query, key, ((1,), (1,)))
             scores = jnp.where((code_ref[...] & kinds) != 0, scores, -1e30)
@@ -308,17 +329,18 @@
             probs = raised * (1.0 / jnp.sum(raised, axis=1, keepdims=True))
             weights = probs.astype(jnp.bfloat16)
             attended = dot(weights, value).astype(jnp.bfloat16)
-            store(att_out, head, attended)
+            rows_ref[4, :, key_lanes] = attended.astype(jnp.float32)
             delta = jnp.sum(grad.astype(jnp.float32) * attended.astype(jnp.float32), axis=1, keepdims=True)
             dprobs = dot(grad, value, ((1,), (1,)))
             dscores = (probs * (dprobs - delta) * SCALE).astype(jnp.bfloat16)
-            store(dq_out, head, dot(dscores, key))
+            rows_ref[5, :, key_lanes] = dot(dscores, key)
             key_part = dot(dscores, query, ((0,), (0,)))
             value_part = dot(weights, grad, ((0,), (0,)))
             for part, lanes in ((key_part, key_lanes), (value_part, value_lanes)):
                 acc[c, :, lanes] = part[0:WP]
                 w_back[c, :, lanes] = part[WP:PAD].astype(jnp.bfloat16)
         on_sides((4, 5), lambda s: back_copy(s, c).start())
+        store((att_out, dq_out), 4, c)
 
     def step_back_columns(c):
         def take(s):
@@ -343,10 +365,10 @@
         got = f_got[c].astype(jnp.float32)
         halves = [jnp.concatenate([got[low : low + RIM], got[PIECE + low : PIECE + low + RIM]], axis=0) for low in (0, RIM)]
         terms = jnp.concatenate(halves, axis=1).astype(jnp.bfloat16)
-        total = (acc[c, 0:CELLS, :] + dot(frames_ref[...], terms)).astype(jnp.bfloat16)
-        total = dot(order_ref[...], total)
-        store(dk_out, c, total[:, 0:HALF], GROUP)
-        store(dv_out, c, total[:, HALF:LANES], GROUP)
+        total = acc[c, 0:CELLS, :] + dot(frames_ref[...], terms)
+        rows_ref[6] = total[:, 0:HALF]
+        rows_ref[7] = total[:, HALF:LANES]
+        store((dk_out, dv_out), 6, c)
 
     def tick(t, carry):
         for step, lag in zip(
@@ -394,17 +416,18 @@
     results = pl.pallas_call(
         kernel,
         out_shape=(shape,) * 4,
-        in_specs=[pl.BlockSpec(memory_space=pltpu.SMEM)] + [vmem] * 12,
+        in_specs=[pl.BlockSpec(memory_space=pltpu.SMEM)] + [vmem] * 10,
         out_specs=(vmem,) * 4,
         scratch_shapes=[pltpu.VMEM((CHUNKS, *dims), jnp.bfloat16) for dims in held]
         + [
-            pltpu.VMEM((2, CHUNKS, PIECE - DIRECT, HALF), jnp.bfloat16),
+            pltpu.VMEM((2, CHUNKS, RELAYED, HALF), jnp.bfloat16),
             pltpu.VMEM((CHUNKS, WP, LANES), jnp.float32),
-            pltpu.SemaphoreType.DMA((16, CHUNKS)),
+            pltpu.VMEM((8, CELLS, HALF), jnp.float32),
+            pltpu.SemaphoreType.DMA((20, CHUNKS)),
             pltpu.SemaphoreType.DMA((14, CHUNKS)),
         ],
         compiler_params=pltpu.CompilerParams(
-            collective_id=0, has_side_effects=True, vmem_limit_bytes=42 * 1024 * 1024
+            collective_id=0, has_side_effects=True, vmem_limit_bytes=60 * 1024 * 1024
         ),
         cost_estimate=pl.CostEstimate(flops=2_500_000_000, bytes_accessed=8_000_000, transcendentals=1_500_000),
     )(extents.T, *flat, *[jnp.asarray(table) for table in tables()])
@@ -413,6 +436,7 @@
         out_shape=(shape,) * 4,
         in_specs=[vmem] * 4,
         out_specs=(vmem,) * 4,
+        compiler_params=pltpu.CompilerParams(vmem_limit_bytes=60 * 1024 * 1024),
         cost_estimate=pl.CostEstimate(flops=0, bytes_accessed=3_600_000, transcendentals=0),
     )(*results)
     return tuple(result.reshape(6, 6, 4, HEADS * HD).transpose(2, 0, 1, 3) for result in results)

time: 100 us -> 90.3 us (0.903)
  local copies, waits for them, and re-layouts: 14.1 us -> 0 us
  Pallas kernels: 84.8 us -> 89.4 us
    unnamed x32 -> x0, local copies, waits for them, and re-layouts: 14.1 us -> none
    pallas_call x1, Pallas kernels: 82.2 us -> 86.8 us  [on_device(): pl.pallas_call(kernel, out_shape=(shape,) * 4, in_specs=[pl.BlockSpec(mem...]
where the time goes in v2:
time: 90.3 us; the launch traced here: 90.1 us
  Pallas kernels  89.4 us (99%)
    pallas_call x1, Pallas kernels, on_device(): pl.pallas_call(kernel, out_shape=(shape,) * 4, in_specs=[pl.BlockSpec(mem...  86.8 us
    pallas_call x1, Pallas kernels, on_device(): pl.pallas_call(hand_out, out_shape=(shape,) * 4, in_specs=[vmem] * 4, out...  2.64 us

profile of v2, /device:TPU:26, one launch (start us, length us, event | category | flops | bytes accessed | tf_op | source)
XLA Modules:
  0.0 90.1 jit_solution(14002783058195406130)
XLA Ops:
  0.6 86.8 %shard_map.138 = (bf16[36,4,1536]{2,1,0:T(4,128)(2,1)}, bf16[36,4,1536]{2,1,0:T(4,128)(2,1)}, bf16[36,4,1536]{2,1,0:T(4,128)(2,1)}, bf16[36,4,1536]{2,1,0:T(4,128)(2,1)}) custom-call(s32[3,12]{1,0:T(4,128)} %bitcast.33, bf16[36,4,1536]{2,1,0:T(4,128)(2,1)} %bitcast.25, bf16[36,4,1536]{2,1,0:T(4,128)(2,1)} %bitcast.26, bf16[36,4,1536]{2,1,0:T(4,128)(2,1)} %bitcast.27, ...), custom_call_target="tpu_custom_call" | custom-call | flops 2500000000 | bytes 8000000 | tf_op jit(solution)/shard_map/pallas_call | solution.py:416
  87.4 2.6 %shard_map.139 = (bf16[36,4,1536]{2,1,0:T(4,128)(2,1)}, bf16[36,4,1536]{2,1,0:T(4,128)(2,1)}, bf16[36,4,1536]{2,1,0:T(4,128)(2,1)}, bf16[36,4,1536]{2,1,0:T(4,128)(2,1)}) custom-call(bf16[36,4,1536]{2,1,0:T(4,128)(2,1)} %get-tuple-element.12.refs_0_, bf16[36,4,1536]{2,1,0:T(4,128)(2,1)} %get-tuple-element.13.refs_1_, ...), custom_call_target="tpu_custom_call" | custom-call | bytes 3600000 | tf_op jit(solution)/shard_map/pallas_call | solution.py:434

commit v3 on v2

--- a/solution.py
+++ b/solution.py
@@ -188,14 +188,14 @@
 
         @pl.when(crossing[s])
         def _():
-            for i, helper in enumerate(helpers[s]):
+            for i, helper in enumerate(helpers[1 - s]):
                 part = src.at[c, pl.ds(here + DIRECT + RELAYED * i, RELAYED)]
                 act(copy(part, by_way.at[way, c], 12 + 4 * way + i, 12 + way, "frame", helper, c))
             act(remote(src.at[c, pl.ds(here, DIRECT)], dst.at[c, pl.ds(there, DIRECT)], number, s, c))
 
     def forward(way, c, act):
         for s, there in ((1, low_mid), (0, high_mid)):
-            for i, helper in enumerate(helpers[1 - s]):
+            for i, helper in enumerate(helpers[s]):
 
                 @pl.when(frame == helper)
                 def _(s=s, there=there, i=i):
@@ -209,7 +209,7 @@
             @pl.when((frame < low_mid) | (frame > high_mid))
             def _():
                 held = by_way.at[way, c]
-                come_from = jnp.where(frame < low_mid, high_mid, low_mid)
+                come_from = jnp.where(frame < low_mid, low_mid, high_mid)
                 copy(held, held, 12 + way, 12 + way, "frame", come_from, c).wait_recv()
 
             forward(way, c, lambda copy: copy.start())

time: 90.3 us -> 79.5 us (0.88)
  Pallas kernels: 89.4 us -> 78.7 us
    pallas_call x1, Pallas kernels: 86.8 us -> 76 us  [on_device(): pl.pallas_call(kernel, out_shape=(shape,) * 4, in_specs=[pl.BlockSpec(mem...]
where the time goes in v3:
time: 79.5 us; the launch traced here: 79.3 us
  Pallas kernels  78.7 us (99%)
    pallas_call x1, Pallas kernels, on_device(): pl.pallas_call(kernel, out_shape=(shape,) * 4, in_specs=[pl.BlockSpec(mem...  76 us
    pallas_call x1, Pallas kernels, on_device(): pl.pallas_call(hand_out, out_shape=(shape,) * 4, in_specs=[vmem] * 4, out...  2.64 us

profile of v3, /device:TPU:26, one launch (start us, length us, event | category | flops | bytes accessed | tf_op | source)
XLA Modules:
  0.0 79.3 jit_solution(17463075352789303852)
XLA Ops:
  0.6 76.0 %shard_map.138 = (bf16[36,4,1536]{2,1,0:T(4,128)(2,1)}, bf16[36,4,1536]{2,1,0:T(4,128)(2,1)}, bf16[36,4,1536]{2,1,0:T(4,128)(2,1)}, bf16[36,4,1536]{2,1,0:T(4,128)(2,1)}) custom-call(s32[3,12]{1,0:T(4,128)} %bitcast.33, bf16[36,4,1536]{2,1,0:T(4,128)(2,1)} %bitcast.25, bf16[36,4,1536]{2,1,0:T(4,128)(2,1)} %bitcast.26, bf16[36,4,1536]{2,1,0:T(4,128)(2,1)} %bitcast.27, ...), custom_call_target="tpu_custom_call" | custom-call | flops 2500000000 | bytes 8000000 | tf_op jit(solution)/shard_map/pallas_call | solution.py:416
  76.7 2.6 %shard_map.139 = (bf16[36,4,1536]{2,1,0:T(4,128)(2,1)}, bf16[36,4,1536]{2,1,0:T(4,128)(2,1)}, bf16[36,4,1536]{2,1,0:T(4,128)(2,1)}, bf16[36,4,1536]{2,1,0:T(4,128)(2,1)}) custom-call(bf16[36,4,1536]{2,1,0:T(4,128)(2,1)} %get-tuple-element.12.refs_0_, bf16[36,4,1536]{2,1,0:T(4,128)(2,1)} %get-tuple-element.13.refs_1_, ...), custom_call_target="tpu_custom_call" | custom-call | bytes 3600000 | tf_op jit(solution)/shard_map/pallas_call | solution.py:434

commit v4 on v3

--- a/solution.py
+++ b/solution.py
@@ -22,7 +22,7 @@
 MESH = pl.DeviceIdType.MESH
 
 FP, FN, HP, HN, WP, WN, PAD, BOX = 144, 224, 304, 400, 496, 672, 848, 896
-LAG = (0, 1, 2, 3, 4, 5, 6, 7, 8)
+LAG = (0, 1, 2, 3, 4, -1, 5, 6, 7, 8)
 RIM, PIECE, DIRECT, RELAYED = 72, 144, 48, 32
 TO_NEXT = ((96, 48, WP), (FP + 48, 32, WP + 48), (FN + 48, 32, WP + 80), (HP + 64, 32, WP + 112), (HN + 64, 32, WP + 144))
 TO_PREV = ((0, 48, WN), (FP, 32, WN + 48), (FN, 32, WN + 80), (HP, 32, WN + 112), (HN, 32, WN + 144))
@@ -75,39 +75,37 @@
     return lax.dot_general(left, right, (sides, ((), ())), preferred_element_type=jnp.float32)
 
 
-def kernel(
-    ext,
-    q_ref,
-    k_ref,
-    v_ref,
-    d_ref,
-    packed_ref,
-    second_ref,
-    second_t_ref,
-    frames_ref,
-    code_ref,
-    side_ref,
-    att_out,
-    dq_out,
-    dk_out,
-    dv_out,
-    box,
-    f_send,
-    f_in,
-    h_send,
-    w_send,
-    w_back,
-    h_back,
-    f_back,
-    w_got,
-    h_got,
-    f_got,
-    by_way,
-    acc,
-    rows_ref,
-    send_sem,
-    recv_sem,
-):
+def kernel(ext, side_ref, *refs):
+    (q_hbm, k_hbm, v_hbm, d_hbm, packed_hbm, second_hbm, second_t_hbm, frames_hbm, code_hbm) = refs[:9]
+    outs = refs[9:13]
+    (q_ref, k_ref, v_ref, d_ref, packed_ref, second_ref, second_t_ref, frames_ref, code_ref) = refs[13:22]
+    att_out, dq_out, dk_out, dv_out = results = refs[22:26]
+    (box, f_send, f_in, h_send, w_send, w_back, h_back, f_back, w_got, h_got, f_got, by_way, acc, rows_ref) = refs[26:40]
+    send_sem, recv_sem, in_sem, out_sem = refs[40:]
+
+    load_first = ((k_hbm, k_ref), (v_hbm, v_ref), (packed_hbm, packed_ref))
+    load_frames = ((second_hbm, second_ref),)
+    load_attend = ((q_hbm, q_ref), (d_hbm, d_ref), (code_hbm, code_ref))
+    load_back = ((second_t_hbm, second_t_ref), (frames_hbm, frames_ref))
+    loads = (*load_first, *load_frames, *load_attend, *load_back)
+
+    def operand(pair):
+        number = [other[1] is pair[1] for other in loads].index(True)
+        return pltpu.make_async_copy(*pair, in_sem.at[number])
+
+    for pair in loads:
+        operand(pair).start()
+
+    def arrive(pairs):
+        for pair in pairs:
+            operand(pair).wait()
+
+    def leave(number, c):
+        if number < 2:
+            return pltpu.make_async_copy(results[number], outs[number], out_sem.at[number, 0])
+        lanes = pl.ds(pl.multiple_of(c * HALF, HALF), HALF)
+        return pltpu.make_async_copy(results[number].at[:, :, lanes], outs[number].at[:, :, lanes], out_sem.at[number, c])
+
     axes = ("frame", "height", "width")
     index = [lax.axis_index(axis) for axis in axes]
     has_prev = [i > 0 for i in index]
@@ -173,8 +171,6 @@
                     pl.semaphore_signal(barrier, inc=1, device_id={"frame": other}, device_id_type=MESH)
 
             greeted = greeted + jnp.where(frame == here, len(others), 0)
-    pl.semaphore_wait(barrier, greeted)
-
     def frame_copies(way, s, c, act):
         src, dst = ((f_send, f_in), (f_back, f_got))[way]
         here, there, number = PIECE * s, PIECE * (1 - s), 6 * way + (s ^ 1)
@@ -283,14 +279,17 @@
 
         regroup(act)
 
-    def step_first(c):
+    def prepare(c):
         key, value = load((k_ref, v_ref), 0, c)
         f_send[c] = dot(packed_ref[...], jnp.concatenate([key, value], axis=0)).astype(jnp.bfloat16)
-        on_sides((0, 1), lambda s: frame_copies(0, s, c, lambda copy: copy.start()))
         box[c, 0:CELLS, 0:HALF] = key
         box[c, 0:CELLS, HALF:LANES] = value
 
+    def step_first(c):
+        on_sides((0, 1), lambda s: frame_copies(0, s, c, lambda copy: copy.start()))
+
     def step_frames(c):
+        pl.when(c == 0)(lambda: arrive(load_frames))
         on_sides((0, 1), lambda s: frames_come(0, s, c))
         got = f_in[c].astype(jnp.float32)
         pad = jnp.zeros((FN - FP - RIM, HALF), jnp.float32)
@@ -310,6 +309,7 @@
         on_sides((4, 5), lambda s: width_copy(s, c).start())
 
     def step_attend(c):
+        pl.when(c == 0)(lambda: arrive(load_attend))
         on_sides((4, 5), lambda s: come(s, c))
         edges = sum(jnp.where(present, 0, 1 << number) for number, _, _, present in sides)
         open_side = (side_ref[0:1, :] & edges) == 0
@@ -341,6 +341,7 @@
                 w_back[c, :, lanes] = part[WP:PAD].astype(jnp.bfloat16)
         on_sides((4, 5), lambda s: back_copy(s, c).start())
         store((att_out, dq_out), 4, c)
+        pl.when(c == CHUNKS - 1)(lambda: [leave(number, 0).start() for number in (0, 1)] and None)
 
     def step_back_columns(c):
         def take(s):
@@ -354,6 +355,7 @@
         on_sides((2, 3), lambda s: back_copy(s, c).start())
 
     def step_back_rows(c):
+        pl.when(c == 0)(lambda: arrive(load_back))
         on_sides((2, 3), lambda s: come_back(s, c))
         acc[c, 0:HP, :] += dot(second_t_ref[...], h_got[c])
         rims = [acc[c, low : low + RIM, HALF * half : HALF * half + HALF] for low in (FP, FN) for half in (0, 1)]
@@ -369,6 +371,8 @@
         rows_ref[6] = total[:, 0:HALF]
         rows_ref[7] = total[:, HALF:LANES]
         store((dk_out, dv_out), 6, c)
+        for number in (2, 3):
+            leave(number, c).start()
 
     def tick(t, carry):
         for step, lag in zip(
@@ -378,6 +382,7 @@
                 step_frames,
                 step_rows,
                 step_attend,
+                prepare,
                 step_back_columns,
                 step_back_rows,
                 functools.partial(step_forward, 1),
@@ -386,12 +391,19 @@
             LAG,
         ):
             c = t - lag
-            pl.when((c >= 0) & (c < CHUNKS))(functools.partial(step, c))
+            pl.when((c >= (1 if lag < 0 else 0)) & (c < CHUNKS))(functools.partial(step, c))
         return carry
 
+    arrive(load_first)
+    prepare(0)
+    pl.semaphore_wait(barrier, greeted)
     lax.fori_loop(0, CHUNKS + LAG[-1], tick, 0)
+    for number in (0, 1):
+        leave(number, 0).wait()
 
     def finish(c, carry):
+        for number in (2, 3):
+            leave(number, c).wait()
         on_sides(range(6), lambda s: all_sent(s, c))
         if shared:
             for way in (0, 1):
@@ -409,33 +421,41 @@
 def on_device(queries, keys, values, out_grad, extents):
     flat = [array.transpose(1, 2, 0, 3).reshape(36, 4, HEADS * HD) for array in (queries, keys, values, out_grad)]
     shape = jax.ShapeDtypeStruct((36, 4, HEADS * HD), jnp.bfloat16)
-    vmem = pl.BlockSpec(memory_space=pltpu.VMEM)
+    vmem, place = pl.BlockSpec(memory_space=pltpu.VMEM), pl.BlockSpec(memory_space=pl.ANY)
     wide, narrow = LANES, HALF
     held = [(BOX, wide), (288, narrow), (288, narrow), (192, wide), (352, wide), (352, wide), (192, wide), (288, narrow)]
     held += [(352, wide), (192, wide), (288, narrow)]
+    *tables_in, side = [jnp.asarray(table) for table in tables()]
+    operands = [*flat, *tables_in]
     results = pl.pallas_call(
         kernel,
         out_shape=(shape,) * 4,
-        in_specs=[pl.BlockSpec(memory_space=pltpu.SMEM)] + [vmem] * 10,
-        out_specs=(vmem,) * 4,
-        scratch_shapes=[pltpu.VMEM((CHUNKS, *dims), jnp.bfloat16) for dims in held]
+        in_specs=[pl.BlockSpec(memory_space=pltpu.SMEM), vmem] + [place] * 9,
+        out_specs=(place,) * 4,
+        scratch_shapes=[pltpu.VMEM(operand.shape, operand.dtype) for operand in operands]
+        + [pltpu.VMEM(shape.shape, shape.dtype)] * 4
+        + [pltpu.VMEM((CHUNKS, *dims), jnp.bfloat16) for dims in held]
         + [
             pltpu.VMEM((2, CHUNKS, RELAYED, HALF), jnp.bfloat16),
             pltpu.VMEM((CHUNKS, WP, LANES), jnp.float32),
             pltpu.VMEM((8, CELLS, HALF), jnp.float32),
             pltpu.SemaphoreType.DMA((20, CHUNKS)),
             pltpu.SemaphoreType.DMA((14, CHUNKS)),
+            pltpu.SemaphoreType.DMA((9,)),
+            pltpu.SemaphoreType.DMA((4, CHUNKS)),
         ],
         compiler_params=pltpu.CompilerParams(
             collective_id=0, has_side_effects=True, vmem_limit_bytes=60 * 1024 * 1024
         ),
         cost_estimate=pl.CostEstimate(flops=2_500_000_000, bytes_accessed=8_000_000, transcendentals=1_500_000),
-    )(extents.T, *flat, *[jnp.asarray(table) for table in tables()])
+    )(extents.T, side, *operands)
+    block = pl.BlockSpec((9, 4, HEADS * HD), lambda i: (i, 0, 0))
     results = pl.pallas_call(
         hand_out,
+        grid=(4,),
         out_shape=(shape,) * 4,
-        in_specs=[vmem] * 4,
-        out_specs=(vmem,) * 4,
+        in_specs=[block] * 4,
+        out_specs=(block,) * 4,
         compiler_params=pltpu.CompilerParams(vmem_limit_bytes=60 * 1024 * 1024),
         cost_estimate=pl.CostEstimate(flops=0, bytes_accessed=3_600_000, transcendentals=0),
     )(*results)

time: 79.5 us -> 78.8 us (level)
  Pallas kernels: 78.7 us -> 77.9 us
    pallas_call x1, Pallas kernels: 76 us -> 74.2 us  [on_device(): pl.pallas_call(kernel, out_shape=(shape,) * 4, in_specs=[pl.BlockSpec(mem...]
    pallas_call x1, Pallas kernels: 2.64 us -> 3.7 us  [on_device(): pl.pallas_call(hand_out, grid=(4,), out_shape=(shape,) * 4, in_specs=[blo...]
where the time goes in v4:
time: 78.8 us; the launch traced here: 78.5 us
  Pallas kernels  77.9 us (99%)
    pallas_call x1, Pallas kernels, on_device(): pl.pallas_call(kernel, out_shape=(shape,) * 4, in_specs=[pl.BlockSpec(mem...  74.2 us
    pallas_call x1, Pallas kernels, on_device(): pl.pallas_call(hand_out, grid=(4,), out_shape=(shape,) * 4, in_specs=[blo...  3.7 us

profile of v4, /device:TPU:26, one launch (start us, length us, event | category | flops | bytes accessed | tf_op | source)
XLA Modules:
  0.0 78.5 jit_solution(5784012325733637882)
XLA Ops:
  0.6 74.2 %shard_map.138 = (bf16[36,4,1536]{2,1,0:T(4,128)(2,1)}, bf16[36,4,1536]{2,1,0:T(4,128)(2,1)}, bf16[36,4,1536]{2,1,0:T(4,128)(2,1)}, bf16[36,4,1536]{2,1,0:T(4,128)(2,1)}) custom-call(s32[3,12]{1,0:T(4,128)} %bitcast.33, s32[8,896]{1,0:T(8,128)} %constant.17.clone.side_ref, bf16[36,4,1536]{2,1,0:T(4,128)(2,1)} %bitcast.25, bf16[36,4,1536]{2,1,0:T(4,128)(2,1)} %bitcast.26, ...), custom_call_target="tpu_custom_call" | custom-call | flops 2500000000 | bytes 8000000 | tf_op jit(solution)/shard_map/pallas_call | solution.py:430
  74.8 3.7 %shard_map.139 = (bf16[36,4,1536]{2,1,0:T(4,128)(2,1)}, bf16[36,4,1536]{2,1,0:T(4,128)(2,1)}, bf16[36,4,1536]{2,1,0:T(4,128)(2,1)}, bf16[36,4,1536]{2,1,0:T(4,128)(2,1)}) custom-call(bf16[36,4,1536]{2,1,0:T(4,128)(2,1)} %get-tuple-element.12.refs_0_, bf16[36,4,1536]{2,1,0:T(4,128)(2,1)} %get-tuple-element.13.refs_1_, ...), custom_call_target="tpu_custom_call" | custom-call | bytes 3600000 | tf_op jit(solution)/shard_map/pallas_call | solution.py:453

commit v5 on v4

--- a/solution.py
+++ b/solution.py
@@ -190,14 +190,13 @@
             act(remote(src.at[c, pl.ds(here, DIRECT)], dst.at[c, pl.ds(there, DIRECT)], number, s, c))
 
     def forward(way, c, act):
-        for s, there in ((1, low_mid), (0, high_mid)):
-            for i, helper in enumerate(helpers[s]):
-
-                @pl.when(frame == helper)
-                def _(s=s, there=there, i=i):
-                    rows = pl.ds(PIECE * s + DIRECT + RELAYED * i, RELAYED)
-                    dst = (f_in, f_got)[way].at[c, rows]
-                    act(copy(by_way.at[way, c], dst, 15 + 4 * way, 6 * way + s, "frame", there, c))
+        low = frame < low_mid
+        s = jnp.where(low, 0, 1)
+        i = jnp.where(low, frame, frame - (high_mid + 1))
+        rows = pl.ds(pl.multiple_of(PIECE * s + DIRECT + RELAYED * i, 16), RELAYED)
+        dst = (f_in, f_got)[way].at[c, rows]
+        there = jnp.where(low, high_mid, low_mid)
+        act(copy(by_way.at[way, c], dst, 15 + 4 * way, 6 * way + s, "frame", there, c))
 
     def step_forward(way, c):
         if shared:
@@ -207,8 +206,7 @@
                 held = by_way.at[way, c]
                 come_from = jnp.where(frame < low_mid, low_mid, high_mid)
                 copy(held, held, 12 + way, 12 + way, "frame", come_from, c).wait_recv()
-
-            forward(way, c, lambda copy: copy.start())
+                forward(way, c, lambda copy: copy.start())
 
     def frames_come(way, s, c):
         got = (f_in, f_got)[way].at[c, pl.ds(PIECE * s, PIECE)]
@@ -256,7 +254,7 @@
                 act((h * 6 + w, h * 6 + 6 + w), pl.ds(pl.multiple_of(w * 24 + 4 * h, 8), 8))
             return carry
 
-        lax.fori_loop(0, 6, column, 0)
+        lax.fori_loop(0, 6, column, 0, unroll=True)
 
     def lanes_of(c):
         return pl.ds(pl.multiple_of(c * HALF, HALF), HALF)
@@ -406,16 +404,32 @@
             leave(number, c).wait()
         on_sides(range(6), lambda s: all_sent(s, c))
         if shared:
-            for way in (0, 1):
-                forward(way, c, lambda copy: copy.wait_send())
+
+            @pl.when((frame < low_mid) | (frame > high_mid))
+            def _():
+                for way in (0, 1):
+                    forward(way, c, lambda copy: copy.wait_send())
+
         return carry
 
     lax.fori_loop(0, CHUNKS, finish, 0)
 
 
 def hand_out(*refs):
+    come, leave = [], []
     for i in range(4):
-        refs[4 + i][...] = refs[i][...]
+        for j in range(2):
+            part = pl.ds(18 * j, 18)
+            held = refs[8 + i].at[part]
+            come.append(pltpu.make_async_copy(refs[i].at[part], held, refs[12].at[i, j]))
+            leave.append(pltpu.make_async_copy(held, refs[4 + i].at[part], refs[13].at[i, j]))
+    for copy in come:
+        copy.start()
+    for first, then in zip(come, leave):
+        first.wait()
+        then.start()
+    for copy in leave:
+        copy.wait()
 
 
 def on_device(queries, keys, values, out_grad, extents):
@@ -449,13 +463,12 @@
         ),
         cost_estimate=pl.CostEstimate(flops=2_500_000_000, bytes_accessed=8_000_000, transcendentals=1_500_000),
     )(extents.T, side, *operands)
-    block = pl.BlockSpec((9, 4, HEADS * HD), lambda i: (i, 0, 0))
     results = pl.pallas_call(
         hand_out,
-        grid=(4,),
         out_shape=(shape,) * 4,
-        in_specs=[block] * 4,
-        out_specs=(block,) * 4,
+        in_specs=[place] * 4,
+        out_specs=(place,) * 4,
+        scratch_shapes=[pltpu.VMEM(shape.shape, shape.dtype)] * 4 + [pltpu.SemaphoreType.DMA((4, 2))] * 2,
         compiler_params=pltpu.CompilerParams(vmem_limit_bytes=60 * 1024 * 1024),
         cost_estimate=pl.CostEstimate(flops=0, bytes_accessed=3_600_000, transcendentals=0),
     )(*results)

time: 78.8 us -> 76.9 us (0.976)
  Pallas kernels: 77.9 us -> 76 us
    pallas_call x1, Pallas kernels: 3.7 us -> 2.38 us  [on_device(): pl.pallas_call(hand_out, out_shape=(shape,) * 4, in_specs=[place] * 4, ou...]
where the time goes in v5:
time: 76.9 us; the launch traced here: 76.7 us
  Pallas kernels  76 us (99%)
    pallas_call x1, Pallas kernels, on_device(): pl.pallas_call(kernel, out_shape=(shape,) * 4, in_specs=[pl.BlockSpec(mem...  73.6 us
    pallas_call x1, Pallas kernels, on_device(): pl.pallas_call(hand_out, out_shape=(shape,) * 4, in_specs=[place] * 4, ou...  2.38 us

profile of v5, /device:TPU:26, one launch (start us, length us, event | category | flops | bytes accessed | tf_op | source)
XLA Modules:
  0.0 76.7 jit_solution(5337589075923625140)
XLA Ops:
  0.6 73.6 %shard_map.138 = (bf16[36,4,1536]{2,1,0:T(4,128)(2,1)}, bf16[36,4,1536]{2,1,0:T(4,128)(2,1)}, bf16[36,4,1536]{2,1,0:T(4,128)(2,1)}, bf16[36,4,1536]{2,1,0:T(4,128)(2,1)}) custom-call(s32[3,12]{1,0:T(4,128)} %bitcast.33, s32[8,896]{1,0:T(8,128)} %constant.17.clone.side_ref, bf16[36,4,1536]{2,1,0:T(4,128)(2,1)} %bitcast.25, bf16[36,4,1536]{2,1,0:T(4,128)(2,1)} %bitcast.26, ...), custom_call_target="tpu_custom_call" | custom-call | flops 2500000000 | bytes 8000000 | tf_op jit(solution)/shard_map/pallas_call | solution.py:444
  74.3 2.4 %shard_map.139 = (bf16[36,4,1536]{2,1,0:T(4,128)(2,1)}, bf16[36,4,1536]{2,1,0:T(4,128)(2,1)}, bf16[36,4,1536]{2,1,0:T(4,128)(2,1)}, bf16[36,4,1536]{2,1,0:T(4,128)(2,1)}) custom-call(bf16[36,4,1536]{2,1,0:T(4,128)(2,1)} %get-tuple-element.12.refs_0_, bf16[36,4,1536]{2,1,0:T(4,128)(2,1)} %get-tuple-element.13.refs_1_, ...), custom_call_target="tpu_custom_call" | custom-call | bytes 3600000 | tf_op jit(solution)/shard_map/pallas_call | solution.py:466

commit v6 on v5

--- a/solution.py
+++ b/solution.py
@@ -13,10 +13,8 @@
 EXT = 2
 TILE = (4, 6, 6)
 CELLS = 144
-GROUP = 2
-CHUNKS = HEADS // GROUP
-HALF = GROUP * HD
-LANES = 2 * HALF
+PAIRS, PAIR = HEADS // 2, 2 * HD
+LANES = 2 * HD
 SCALE = HD**-0.5
 LOG2E = 1.4426950408889634
 MESH = pl.DeviceIdType.MESH
@@ -100,11 +98,11 @@
         for pair in pairs:
             operand(pair).wait()
 
-    def leave(number, c):
+    def leave(number, j):
         if number < 2:
             return pltpu.make_async_copy(results[number], outs[number], out_sem.at[number, 0])
-        lanes = pl.ds(pl.multiple_of(c * HALF, HALF), HALF)
-        return pltpu.make_async_copy(results[number].at[:, :, lanes], outs[number].at[:, :, lanes], out_sem.at[number, c])
+        lanes = pl.ds(pl.multiple_of(j * PAIR, PAIR), PAIR)
+        return pltpu.make_async_copy(results[number].at[:, :, lanes], outs[number].at[:, :, lanes], out_sem.at[number, j])
 
     axes = ("frame", "height", "width")
     index = [lax.axis_index(axis) for axis in axes]
@@ -135,7 +133,7 @@
         _, axis, other, _ = sides[s]
         return copy(src, dst, number, number, axis, other, c)
 
-    box[:, PAD:BOX, :] = jnp.zeros((CHUNKS, BOX - PAD, LANES), jnp.bfloat16)
+    box[:, PAD:BOX, :] = jnp.zeros((HEADS, BOX - PAD, LANES), jnp.bfloat16)
     backs = ((h_back, h_got, 96), (w_back, w_got, 176))
     regions = ((FP, FN), (FN, HP), (HP, HN), (HN, WP), (WP, WN), (WN, PAD))
     for (number, _, _, present), (low, high) in zip(sides, regions):
@@ -145,12 +143,12 @@
             if number < 2:
                 at = PIECE * number
                 for got in (f_in, f_got):
-                    got[:, at : at + PIECE, :] = jnp.zeros((CHUNKS, PIECE, HALF), jnp.bfloat16)
+                    got[:, at : at + PIECE, :] = jnp.zeros((HEADS, PIECE, HD), jnp.bfloat16)
             else:
-                box[:, low:high, :] = jnp.zeros((CHUNKS, high - low, LANES), jnp.bfloat16)
+                box[:, low:high, :] = jnp.zeros((HEADS, high - low, LANES), jnp.bfloat16)
             if number in (2, 3):
                 at = 96 * (number - 2)
-                h_got[:, at : at + 96, :] = jnp.zeros((CHUNKS, 96, LANES), jnp.bfloat16)
+                h_got[:, at : at + 96, :] = jnp.zeros((HEADS, 96, LANES), jnp.bfloat16)
 
     barrier = pltpu.get_barrier_semaphore()
     for _, axis, other, present in sides:
@@ -198,15 +196,16 @@
         there = jnp.where(low, high_mid, low_mid)
         act(copy(by_way.at[way, c], dst, 15 + 4 * way, 6 * way + s, "frame", there, c))
 
-    def step_forward(way, c):
+    def step_forward(way, j):
         if shared:
 
             @pl.when((frame < low_mid) | (frame > high_mid))
             def _():
-                held = by_way.at[way, c]
                 come_from = jnp.where(frame < low_mid, low_mid, high_mid)
-                copy(held, held, 12 + way, 12 + way, "frame", come_from, c).wait_recv()
-                forward(way, c, lambda copy: copy.start())
+                for c in (2 * j, 2 * j + 1):
+                    held = by_way.at[way, c]
+                    copy(held, held, 12 + way, 12 + way, "frame", come_from, c).wait_recv()
+                    forward(way, c, lambda copy: copy.start())
 
     def frames_come(way, s, c):
         got = (f_in, f_got)[way].at[c, pl.ds(PIECE * s, PIECE)]
@@ -256,32 +255,41 @@
 
         lax.fori_loop(0, 6, column, 0, unroll=True)
 
-    def lanes_of(c):
-        return pl.ds(pl.multiple_of(c * HALF, HALF), HALF)
-
-    def load(refs, slot, c):
+    def lanes_of(j):
+        return pl.ds(pl.multiple_of(j * PAIR, PAIR), PAIR)
+
+    def load(refs, slot, j):
         def act(places, rows):
             for n, ref in enumerate(refs):
-                pair = [ref[place, :, lanes_of(c)].astype(jnp.float32) for place in places]
+                pair = [ref[place, :, lanes_of(j)].astype(jnp.float32) for place in places]
                 rows_ref[slot + n, rows, :] = jnp.concatenate(pair, axis=0)
 
         regroup(act)
         return [rows_ref[slot + n].astype(jnp.bfloat16) for n in range(len(refs))]
 
-    def store(refs, slot, c):
+    def store(refs, slot, j):
         def act(places, rows):
             for n, ref in enumerate(refs):
                 pair = rows_ref[slot + n, rows, :]
                 for k, place in enumerate(places):
-                    ref[place, :, lanes_of(c)] = pair[4 * k : 4 * k + 4].astype(jnp.bfloat16)
+                    ref[place, :, lanes_of(j)] = pair[4 * k : 4 * k + 4].astype(jnp.bfloat16)
 
         regroup(act)
 
-    def prepare(c):
-        key, value = load((k_ref, v_ref), 0, c)
-        f_send[c] = dot(packed_ref[...], jnp.concatenate([key, value], axis=0)).astype(jnp.bfloat16)
-        box[c, 0:CELLS, 0:HALF] = key
-        box[c, 0:CELLS, HALF:LANES] = value
+    def prepare(j):
+        keys, values = load((k_ref, v_ref), 0, j)
+        for g in (0, 1):
+            key, value = keys[:, g * HD : g * HD + HD], values[:, g * HD : g * HD + HD]
+            f_send[2 * j + g] = dot(packed_ref[...], jnp.concatenate([key, value], axis=0)).astype(jnp.bfloat16)
+            box[2 * j + g, 0:CELLS, 0:HD] = key
+            box[2 * j + g, 0:CELLS, HD:LANES] = value
+
+    def each(step):
+        def both(j):
+            step(2 * j)
+            step(2 * j + 1)
+
+        return both
 
     def step_first(c):
         on_sides((0, 1), lambda s: frame_copies(0, s, c, lambda copy: copy.start()))
@@ -290,11 +298,11 @@
         pl.when(c == 0)(lambda: arrive(load_frames))
         on_sides((0, 1), lambda s: frames_come(0, s, c))
         got = f_in[c].astype(jnp.float32)
-        pad = jnp.zeros((FN - FP - RIM, HALF), jnp.float32)
+        pad = jnp.zeros((FN - FP - RIM, HD), jnp.float32)
         for half in (0, 1):
             low = RIM * half
             rims = [got[low : low + RIM], pad, got[PIECE + low : PIECE + low + RIM], pad]
-            box[c, FP:HP, HALF * half : HALF * half + HALF] = jnp.concatenate(rims, axis=0).astype(jnp.bfloat16)
+            box[c, FP:HP, HD * half : HD * half + HD] = jnp.concatenate(rims, axis=0).astype(jnp.bfloat16)
         h_send[c] = dot(second_ref[...], box[c, 0:HP, :]).astype(jnp.bfloat16)
         on_sides((2, 3), lambda s: height_copy(s, c).start())
 
@@ -306,20 +314,20 @@
                 w_send[c, at : at + count, :] = box[c, start : start + count, :]
         on_sides((4, 5), lambda s: width_copy(s, c).start())
 
-    def step_attend(c):
-        pl.when(c == 0)(lambda: arrive(load_attend))
-        on_sides((4, 5), lambda s: come(s, c))
+    def step_attend(j):
+        pl.when(j == 0)(lambda: arrive(load_attend))
+        for c in (2 * j, 2 * j + 1):
+            on_sides((4, 5), lambda s: come(s, c))
         edges = sum(jnp.where(present, 0, 1 << number) for number, _, _, present in sides)
         open_side = (side_ref[0:1, :] & edges) == 0
-        queries, grads = load((q_ref, d_ref), 2, c)
-        for g in range(GROUP):
-            head = c * GROUP + g
-            key_lanes = slice(g * HD, g * HD + HD)
-            value_lanes = slice(HALF + g * HD, HALF + g * HD + HD)
-            kind = (15 * ext[0, head] - 14) * (3 * ext[1, head] - 2) * ext[2, head]
+        queries, grads = load((q_ref, d_ref), 2, j)
+        for g in (0, 1):
+            c = 2 * j + g
+            lanes = slice(g * HD, g * HD + HD)
+            kind = (15 * ext[0, c] - 14) * (3 * ext[1, c] - 2) * ext[2, c]
             kinds = jnp.where(open_side, kind, 0)
-            query, grad = queries[:, key_lanes], grads[:, key_lanes]
-            key, value = box[c, :, key_lanes], box[c, :, value_lanes]
+            query, grad = queries[:, lanes], grads[:, lanes]
+            key, value = box[c, :, 0:HD], box[c, :, HD:LANES]
             scores = dot(query, key, ((1,), (1,)))
             scores = jnp.where((code_ref[...] & kinds) != 0, scores, -1e30)
             top = jnp.max(scores, axis=1, keepdims=True)
@@ -327,19 +335,20 @@
             probs = raised * (1.0 / jnp.sum(raised, axis=1, keepdims=True))
             weights = probs.astype(jnp.bfloat16)
             attended = dot(weights, value).astype(jnp.bfloat16)
-            rows_ref[4, :, key_lanes] = attended.astype(jnp.float32)
+            rows_ref[4, :, lanes] = attended.astype(jnp.float32)
             delta = jnp.sum(grad.astype(jnp.float32) * attended.astype(jnp.float32), axis=1, keepdims=True)
             dprobs = dot(grad, value, ((1,), (1,)))
             dscores = (probs * (dprobs - delta) * SCALE).astype(jnp.bfloat16)
-            rows_ref[5, :, key_lanes] = dot(dscores, key)
+            rows_ref[5, :, lanes] = dot(dscores, key)
             key_part = dot(dscores, query, ((0,), (0,)))
             value_part = dot(weights, grad, ((0,), (0,)))
-            for part, lanes in ((key_part, key_lanes), (value_part, value_lanes)):
-                acc[c, :, lanes] = part[0:WP]
-                w_back[c, :, lanes] = part[WP:PAD].astype(jnp.bfloat16)
-        on_sides((4, 5), lambda s: back_copy(s, c).start())
-        store((att_out, dq_out), 4, c)
-        pl.when(c == CHUNKS - 1)(lambda: [leave(number, 0).start() for number in (0, 1)] and None)
+            for part, place in ((key_part, slice(0, HD)), (value_part, slice(HD, LANES))):
+                acc[c, :, place] = part[0:WP]
+                w_back[c, :, place] = part[WP:PAD].astype(jnp.bfloat16)
+        for c in (2 * j, 2 * j + 1):
+            on_sides((4, 5), lambda s: back_copy(s, c).start())
+        store((att_out, dq_out), 4, j)
+        pl.when(j == PAIRS - 1)(lambda: [leave(number, 0).start() for number in (0, 1)] and None)
 
     def step_back_columns(c):
         def take(s):
@@ -356,52 +365,58 @@
         pl.when(c == 0)(lambda: arrive(load_back))
         on_sides((2, 3), lambda s: come_back(s, c))
         acc[c, 0:HP, :] += dot(second_t_ref[...], h_got[c])
-        rims = [acc[c, low : low + RIM, HALF * half : HALF * half + HALF] for low in (FP, FN) for half in (0, 1)]
+        rims = [acc[c, low : low + RIM, HD * half : HD * half + HD] for low in (FP, FN) for half in (0, 1)]
         f_back[c] = jnp.concatenate(rims, axis=0).astype(jnp.bfloat16)
         on_sides((0, 1), lambda s: frame_copies(1, s, c, lambda copy: copy.start()))
 
-    def step_back_frames(c):
-        on_sides((0, 1), lambda s: frames_come(1, s, c))
-        got = f_got[c].astype(jnp.float32)
-        halves = [jnp.concatenate([got[low : low + RIM], got[PIECE + low : PIECE + low + RIM]], axis=0) for low in (0, RIM)]
-        terms = jnp.concatenate(halves, axis=1).astype(jnp.bfloat16)
-        total = acc[c, 0:CELLS, :] + dot(frames_ref[...], terms)
-        rows_ref[6] = total[:, 0:HALF]
-        rows_ref[7] = total[:, HALF:LANES]
-        store((dk_out, dv_out), 6, c)
+    def step_back_frames(j):
+        for g in (0, 1):
+            c = 2 * j + g
+            on_sides((0, 1), lambda s: frames_come(1, s, c))
+            got = f_got[c].astype(jnp.float32)
+            halves = [
+                jnp.concatenate([got[low : low + RIM], got[PIECE + low : PIECE + low + RIM]], axis=0) for low in (0, RIM)
+            ]
+            terms = jnp.concatenate(halves, axis=1).astype(jnp.bfloat16)
+            total = acc[c, 0:CELLS, :] + dot(frames_ref[...], terms)
+            rows_ref[6, :, g * HD : g * HD + HD] = total[:, 0:HD]
+            rows_ref[7, :, g * HD : g * HD + HD] = total[:, HD:LANES]
+        store((dk_out, dv_out), 6, j)
         for number in (2, 3):
-            leave(number, c).start()
+            leave(number, j).start()
 
     def tick(t, carry):
         for step, lag in zip(
             (
-                step_first,
+                each(step_first),
                 functools.partial(step_forward, 0),
-                step_frames,
-                step_rows,
+                each(step_frames),
+                each(step_rows),
                 step_attend,
                 prepare,
-                step_back_columns,
-                step_back_rows,
+                each(step_back_columns),
+                each(step_back_rows),
                 functools.partial(step_forward, 1),
                 step_back_frames,
             ),
             LAG,
         ):
-            c = t - lag
-            pl.when((c >= (1 if lag < 0 else 0)) & (c < CHUNKS))(functools.partial(step, c))
+            j = t - lag
+            pl.when((j >= (1 if lag < 0 else 0)) & (j < PAIRS))(functools.partial(step, j))
         return carry
 
     arrive(load_first)
     prepare(0)
     pl.semaphore_wait(barrier, greeted)
-    lax.fori_loop(0, CHUNKS + LAG[-1], tick, 0)
+    lax.fori_loop(0, PAIRS + LAG[-1], tick, 0)
     for number in (0, 1):
         leave(number, 0).wait()
 
+    for number in (2, 3):
+        for j in range(PAIRS):
+            leave(number, j).wait()
+
     def finish(c, carry):
-        for number in (2, 3):
-            leave(number, c).wait()
         on_sides(range(6), lambda s: all_sent(s, c))
         if shared:
 
@@ -412,7 +427,7 @@
 
         return carry
 
-    lax.fori_loop(0, CHUNKS, finish, 0)
+    lax.fori_loop(0, HEADS, finish, 0)
 
 
 def hand_out(*refs):
@@ -436,7 +451,7 @@
     flat = [array.transpose(1, 2, 0, 3).reshape(36, 4, HEADS * HD) for array in (queries, keys, values, out_grad)]
     shape = jax.ShapeDtypeStruct((36, 4, HEADS * HD), jnp.bfloat16)
     vmem, place = pl.BlockSpec(memory_space=pltpu.VMEM), pl.BlockSpec(memory_space=pl.ANY)
-    wide, narrow = LANES, HALF
+    wide, narrow = LANES, HD
     held = [(BOX, wide), (288, narrow), (288, narrow), (192, wide), (352, wide), (352, wide), (192, wide), (288, narrow)]
     held += [(352, wide), (192, wide), (288, narrow)]
     *tables_in, side = [jnp.asarray(table) for table in tables()]
@@ -448,15 +463,15 @@
         out_specs=(place,) * 4,
         scratch_shapes=[pltpu.VMEM(operand.shape, operand.dtype) for operand in operands]
         + [pltpu.VMEM(shape.shape, shape.dtype)] * 4
-        + [pltpu.VMEM((CHUNKS, *dims), jnp.bfloat16) for dims in held]
+        + [pltpu.VMEM((HEADS, *dims), jnp.bfloat16) for dims in held]
         + [
-            pltpu.VMEM((2, CHUNKS, RELAYED, HALF), jnp.bfloat16),
-            pltpu.VMEM((CHUNKS, WP, LANES), jnp.float32),
-            pltpu.VMEM((8, CELLS, HALF), jnp.float32),
-            pltpu.SemaphoreType.DMA((20, CHUNKS)),
-            pltpu.SemaphoreType.DMA((14, CHUNKS)),
+            pltpu.VMEM((2, HEADS, RELAYED, HD), jnp.bfloat16),
+            pltpu.VMEM((HEADS, WP, LANES), jnp.float32),
+            pltpu.VMEM((8, CELLS, PAIR), jnp.float32),
+            pltpu.SemaphoreType.DMA((20, HEADS)),
+            pltpu.SemaphoreType.DMA((14, HEADS)),
             pltpu.SemaphoreType.DMA((9,)),
-            pltpu.SemaphoreType.DMA((4, CHUNKS)),
+            pltpu.SemaphoreType.DMA((4, PAIRS)),
         ],
         compiler_params=pltpu.CompilerParams(
             collective_id=0, has_side_effects=True, vmem_limit_bytes=60 * 1024 * 1024

time: 76.9 us -> 76.6 us (level)
  no operation moved by 1% of the time
where the time goes in v6:
time: 76.6 us; the launch traced here: 76.4 us
  Pallas kernels  75.8 us (99%)
    pallas_call x1, Pallas kernels, on_device(): pl.pallas_call(kernel, out_shape=(shape,) * 4, in_specs=[pl.BlockSpec(mem...  73.4 us
    pallas_call x1, Pallas kernels, on_device(): pl.pallas_call(hand_out, out_shape=(shape,) * 4, in_specs=[place] * 4, ou...  2.38 us

profile of v6, /device:TPU:26, one launch (start us, length us, event | category | flops | bytes accessed | tf_op | source)
XLA Modules:
  0.0 76.4 jit_solution(5581045085623658260)
XLA Ops:
  0.6 73.4 %shard_map.138 = (bf16[36,4,1536]{2,1,0:T(4,128)(2,1)}, bf16[36,4,1536]{2,1,0:T(4,128)(2,1)}, bf16[36,4,1536]{2,1,0:T(4,128)(2,1)}, bf16[36,4,1536]{2,1,0:T(4,128)(2,1)}) custom-call(s32[3,12]{1,0:T(4,128)} %bitcast.33, s32[8,896]{1,0:T(8,128)} %constant.17.clone.side_ref, bf16[36,4,1536]{2,1,0:T(4,128)(2,1)} %bitcast.25, bf16[36,4,1536]{2,1,0:T(4,128)(2,1)} %bitcast.26, ...), custom_call_target="tpu_custom_call" | custom-call | flops 2500000000 | bytes 8000000 | tf_op jit(solution)/shard_map/pallas_call | solution.py:459
  74.0 2.4 %shard_map.139 = (bf16[36,4,1536]{2,1,0:T(4,128)(2,1)}, bf16[36,4,1536]{2,1,0:T(4,128)(2,1)}, bf16[36,4,1536]{2,1,0:T(4,128)(2,1)}, bf16[36,4,1536]{2,1,0:T(4,128)(2,1)}) custom-call(bf16[36,4,1536]{2,1,0:T(4,128)(2,1)} %get-tuple-element.12.refs_0_, bf16[36,4,1536]{2,1,0:T(4,128)(2,1)} %get-tuple-element.13.refs_1_, ...), custom_call_target="tpu_custom_call" | custom-call | bytes 3600000 | tf_op jit(solution)/shard_map/pallas_call | solution.py:481

commit v7 on v5

--- a/solution.py
+++ b/solution.py
@@ -22,7 +22,7 @@
 MESH = pl.DeviceIdType.MESH
 
 FP, FN, HP, HN, WP, WN, PAD, BOX = 144, 224, 304, 400, 496, 672, 848, 896
-LAG = (0, 1, 2, 3, 4, -1, 5, 6, 7, 8)
+LAG = (1, 2, 3, 0, 4, -1, 7, 5, 6, 8)
 RIM, PIECE, DIRECT, RELAYED = 72, 144, 48, 32
 TO_NEXT = ((96, 48, WP), (FP + 48, 32, WP + 48), (FN + 48, 32, WP + 80), (HP + 64, 32, WP + 112), (HN + 64, 32, WP + 144))
 TO_PREV = ((0, 48, WN), (FP, 32, WN + 48), (FN, 32, WN + 80), (HP, 32, WN + 112), (HN, 32, WN + 144))
@@ -375,15 +375,15 @@
     def tick(t, carry):
         for step, lag in zip(
             (
-                step_first,
                 functools.partial(step_forward, 0),
                 step_frames,
                 step_rows,
+                step_first,
                 step_attend,
                 prepare,
+                functools.partial(step_forward, 1),
                 step_back_columns,
                 step_back_rows,
-                functools.partial(step_forward, 1),
                 step_back_frames,
             ),
             LAG,

time: 76.9 us -> 79.7 us (1.036)
  Pallas kernels: 76 us -> 78.8 us
    pallas_call x1, Pallas kernels: 73.6 us -> 76.4 us  [on_device(): pl.pallas_call(kernel, out_shape=(shape,) * 4, in_specs=[pl.BlockSpec(mem...]
where the time goes in v7:
time: 79.7 us; the launch traced here: 79.4 us
  Pallas kernels  78.8 us (99%)
    pallas_call x1, Pallas kernels, on_device(): pl.pallas_call(kernel, out_shape=(shape,) * 4, in_specs=[pl.BlockSpec(mem...  76.4 us
    pallas_call x1, Pallas kernels, on_device(): pl.pallas_call(hand_out, out_shape=(shape,) * 4, in_specs=[place] * 4, ou...  2.38 us

profile of v7, /device:TPU:26, one launch (start us, length us, event | category | flops | bytes accessed | tf_op | source)
XLA Modules:
  0.0 79.4 jit_solution(11379537278330551588)
XLA Ops:
  0.6 76.4 %shard_map.138 = (bf16[36,4,1536]{2,1,0:T(4,128)(2,1)}, bf16[36,4,1536]{2,1,0:T(4,128)(2,1)}, bf16[36,4,1536]{2,1,0:T(4,128)(2,1)}, bf16[36,4,1536]{2,1,0:T(4,128)(2,1)}) custom-call(s32[3,12]{1,0:T(4,128)} %bitcast.33, s32[8,896]{1,0:T(8,128)} %constant.17.clone.side_ref, bf16[36,4,1536]{2,1,0:T(4,128)(2,1)} %bitcast.25, bf16[36,4,1536]{2,1,0:T(4,128)(2,1)} %bitcast.26, ...), custom_call_target="tpu_custom_call" | custom-call | flops 2500000000 | bytes 8000000 | tf_op jit(solution)/shard_map/pallas_call | solution.py:444
  77.0 2.4 %shard_map.139 = (bf16[36,4,1536]{2,1,0:T(4,128)(2,1)}, bf16[36,4,1536]{2,1,0:T(4,128)(2,1)}, bf16[36,4,1536]{2,1,0:T(4,128)(2,1)}, bf16[36,4,1536]{2,1,0:T(4,128)(2,1)}) custom-call(bf16[36,4,1536]{2,1,0:T(4,128)(2,1)} %get-tuple-element.12.refs_0_, bf16[36,4,1536]{2,1,0:T(4,128)(2,1)} %get-tuple-element.13.refs_1_, ...), custom_call_target="tpu_custom_call" | custom-call | bytes 3600000 | tf_op jit(solution)/shard_map/pallas_call | solution.py:466

commit v8 on v5

--- a/solution.py
+++ b/solution.py
@@ -22,7 +22,7 @@
 MESH = pl.DeviceIdType.MESH
 
 FP, FN, HP, HN, WP, WN, PAD, BOX = 144, 224, 304, 400, 496, 672, 848, 896
-LAG = (0, 1, 2, 3, 4, -1, 5, 6, 7, 8)
+LAG = (-1, 0, 2, 3, 4, -2, 5, 6, 7, 8)
 RIM, PIECE, DIRECT, RELAYED = 72, 144, 48, 32
 TO_NEXT = ((96, 48, WP), (FP + 48, 32, WP + 48), (FN + 48, 32, WP + 80), (HP + 64, 32, WP + 112), (HN + 64, 32, WP + 144))
 TO_PREV = ((0, 48, WN), (FP, 32, WN + 48), (FN, 32, WN + 80), (HP, 32, WN + 112), (HN, 32, WN + 144))
@@ -389,12 +389,14 @@
             LAG,
         ):
             c = t - lag
-            pl.when((c >= (1 if lag < 0 else 0)) & (c < CHUNKS))(functools.partial(step, c))
+            pl.when((c >= max(0, -lag)) & (c < CHUNKS))(functools.partial(step, c))
         return carry
 
     arrive(load_first)
     prepare(0)
     pl.semaphore_wait(barrier, greeted)
+    step_first(0)
+    prepare(1)
     lax.fori_loop(0, CHUNKS + LAG[-1], tick, 0)
     for number in (0, 1):
         leave(number, 0).wait()

time: 76.9 us -> 76.6 us (level)
  no operation moved by 1% of the time
where the time goes in v8:
time: 76.6 us; the launch traced here: 76 us
  Pallas kernels  75.4 us (98%)
    pallas_call x1, Pallas kernels, on_device(): pl.pallas_call(kernel, out_shape=(shape,) * 4, in_specs=[pl.BlockSpec(mem...  73 us
    pallas_call x1, Pallas kernels, on_device(): pl.pallas_call(hand_out, out_shape=(shape,) * 4, in_specs=[place] * 4, ou...  2.38 us

profile of v8, /device:TPU:26, one launch (start us, length us, event | category | flops | bytes accessed | tf_op | source)
XLA Modules:
  0.0 76.0 jit_solution(2284825039396733051)
XLA Ops:
  0.6 73.0 %shard_map.138 = (bf16[36,4,1536]{2,1,0:T(4,128)(2,1)}, bf16[36,4,1536]{2,1,0:T(4,128)(2,1)}, bf16[36,4,1536]{2,1,0:T(4,128)(2,1)}, bf16[36,4,1536]{2,1,0:T(4,128)(2,1)}) custom-call(s32[3,12]{1,0:T(4,128)} %bitcast.33, s32[8,896]{1,0:T(8,128)} %constant.17.clone.side_ref, bf16[36,4,1536]{2,1,0:T(4,128)(2,1)} %bitcast.25, bf16[36,4,1536]{2,1,0:T(4,128)(2,1)} %bitcast.26, ...), custom_call_target="tpu_custom_call" | custom-call | flops 2500000000 | bytes 8000000 | tf_op jit(solution)/shard_map/pallas_call | solution.py:446
  73.6 2.4 %shard_map.139 = (bf16[36,4,1536]{2,1,0:T(4,128)(2,1)}, bf16[36,4,1536]{2,1,0:T(4,128)(2,1)}, bf16[36,4,1536]{2,1,0:T(4,128)(2,1)}, bf16[36,4,1536]{2,1,0:T(4,128)(2,1)}) custom-call(bf16[36,4,1536]{2,1,0:T(4,128)(2,1)} %get-tuple-element.12.refs_0_, bf16[36,4,1536]{2,1,0:T(4,128)(2,1)} %get-tuple-element.13.refs_1_, ...), custom_call_target="tpu_custom_call" | custom-call | bytes 3600000 | tf_op jit(solution)/shard_map/pallas_call | solution.py:468
